TPU v7x, 256 devices: a whole 4x4x8 slice. The times are simulated.
256 devices in a mesh: dp: 8 (over x, core), cent: 32 (over y, z).
Axes of the slice: x: 4, y: 4, z: 8, core: 2. Of those that a mesh axis runs over, the one named last changes fastest.
Arguments:
- embeddings: bfloat16 [8192, 4096], P('dp', 'cent'), may hold values from -6 to 6
- centroids: bfloat16 [16384, 4096], P('cent'), may hold values from -0.1875 to 0.1875
- assignment: int32 [8192], P('dp'), may hold values from 0 to 16383, as said below
- prior_counts: int32 [16384], P('cent'), may hold values from 1 to 4
Outputs:
- top_score: float32 [8192], P('dp')
- updated: float32 [4096, 16384], P('dp', 'cent')
Inputs may be any that keep to these rules, and one draw needn't show every extreme that they name: `assignment`: cluster k belongs to index k // 512 of cent. Among the 1024 rows of one index of dp, at most 64 have clusters that belong to one index of cent, and in every such block of rows some index of cent gets exactly 64 of them.
All inputs are finite; a program needn't handle non-finite values.
Results may differ from a plain program's by a relative error of at most 0.0003.
Values may be sent and summed in bfloat16 or wider, within the bound.
A program may use at most 64 MiB of HBM per device.

v0:
```python
import jax
import jax.numpy as jnp
from jax import lax
from jax.sharding import PartitionSpec as P


def on_device(embeddings, centroids, assignment, prior_counts):
    whole = lax.all_gather(embeddings, "cent", axis=1, tiled=True)
    width = centroids.shape[0]
    half_norm = 0.5 * jnp.sum(jnp.square(centroids.astype(jnp.float32)), axis=1)
    score = (
        lax.dot_general(
            whole, centroids, (((1,), (1,)), ((), ())), preferred_element_type=jnp.float32
        )
        - half_norm[None, :]
    )
    top_score = lax.pmax(jnp.max(score, axis=1), "cent")
    owned = lax.axis_index("cent") * width + jnp.arange(width, dtype=jnp.int32)
    slice_width = whole.shape[1] // lax.axis_size("dp")
    match = assignment[:, None] == owned[None, :]
    onehot = match.astype(jnp.bfloat16)
    sums = lax.psum_scatter(
        lax.dot_general(
            whole, onehot, (((0,), (0,)), ((), ())), preferred_element_type=jnp.float32
        ),
        "dp",
        scatter_dimension=0,
        tiled=True,
    )
    counts = lax.psum(jnp.sum(match, axis=0, dtype=jnp.float32), "dp")
    own_slice = (
        lax.dynamic_slice_in_dim(centroids, lax.axis_index("dp") * slice_width, slice_width, 1)
        .astype(jnp.float32)
        .T
    )
    prior = prior_counts.astype(jnp.float32)
    updated = (prior[None, :] * own_slice + sums) / (prior + counts)[None, :]
    return (top_score, updated)


def solution(mesh):
    placed = (P("dp", "cent"), P("cent", None), P("dp"), P("cent"))
    return jax.shard_map(
        on_device, mesh=mesh, in_specs=placed, out_specs=(P("dp"), P("dp", "cent")), check_vma=False
    )
```

profile of v0, /device:TPU:0, one launch (start us, length us, event | category | flops | bytes accessed | tf_op | source)
XLA Modules:
  0.0 234.0 jit_solution(10257634500430991957)
XLA Ops:
  7.2 0.0 all-gather.2.cloned.1.call-start
  7.2 0.7 all-gather.2.cloned.1.call-update
  7.9 0.0 reduce-scatter.2.cloned.1.call-start
  8.0 107.5 %all-gather.2.cloned.1.call-done = bf16[1024,4096]{1,0:T(8,128)(2,1)} async-done(((bf16[1024,128]{1,0:T(8,128)(2,1)}), bf16[1024,4096]{1,0:T(8,128)(2,1)}) %all-gather.2.cloned.1.call-update) | async-done | bytes 8388624 | tf_op jit(solution)/shard_map/all_gather | solution.py:8
  115.4 10.4 %convolution_bitcast_fusion = f32[4096,512]{0,1:T(8,128)} fusion(bf16[1024,4096]{1,0:T(8,128)(2,1)} %all-gather.2.cloned.1.call-done, s32[512]{0:T(512)S(1)} %iota_add_fusion, s32[1024]{0:T(1024)} %param.6), kind=kOutput, calls=%fused_computation.1 | convolution fusion | flops 4295491584 | bytes 16783360 | tf_op jit(solution)/shard_map/dot_general | solution.py:23
  125.8 0.0 copy-start.1
  125.8 0.0 copy-start.2
  125.8 0.0 reduce-scatter.2.cloned.1.call-update
  125.8 0.6 copy-done.1
  126.5 0.0 copy-done.2
  126.5 0.3 fusion.2
  126.8 12.4 %psum.7 = f32[512]{0:T(512)S(1)} all-reduce(f32[512]{0:T(512)S(1)} %fusion.2), channel_id=1, replica_groups=mesh['dp'=8,'cent'=32] {'dp'}, use_global_device_ids=true, to_apply=%region_5.0 | all-reduce | flops 512 | bytes 4096 | tf_op jit(solution)/shard_map/psum | solution.py:30
  139.2 0.0 copy-start
  139.2 3.3 %multiply_reduce_fusion = f32[512]{0:T(512)S(1)} fusion(bf16[512,4096]{1,0:T(8,128)(2,1)} %param.5), kind=kLoop, calls=%fused_computation | loop fusion | flops 6290944 | bytes 4196352 | tf_op jit(solution)/shard_map/reduce_sum | solution.py:10
  142.5 0.3 copy-done
  142.8 8.1 %subtract_reduce_fusion = f32[1024]{0:T(1024)S(1)} fusion(bf16[1024,4096]{1,0:T(8,128)(2,1)} %all-gather.2.cloned.1.call-done, bf16[512,4096]{1,0:T(8,128)(2,1)S(1)} %copy-done, f32[512]{0:T(512)S(1)} %broadcast_multiply_fusion), kind=kOutput, calls=%fused_computation.6 | convolution fusion | flops 4296014848 | bytes 12589056 | tf_op jit(solution)/shard_map/dot_general | solution.py:12
  150.9 73.4 %pmax.7 = f32[1024]{0:T(1024)} all-reduce(f32[1024]{0:T(1024)S(1)} %subtract_reduce_fusion), channel_id=1, replica_groups=mesh['dp'=8,'cent'=32] {'cent'}, use_global_device_ids=true, to_apply=%region_2.0 | all-reduce | flops 1024 | bytes 8192 | tf_op jit(solution)/shard_map/pmax | solution.py:17
  224.2 0.0 reduce-scatter.2.cloned.1.call-done
  224.2 1.6 fusion.3
  225.8 1.3 copy.7
  (4 shorter events, 0.0 us)
Async XLA Ops:
  7.2 108.3 %all-gather.2.cloned.1.call-start = ((), (), s32[]{:S(2)}) async-start(), calls=%async_computation.1 | async-start | bytes 8650752 | tf_op jit(solution)/shard_map/all_gather | solution.py:8
  7.9 216.3 %reduce-scatter.2.cloned.1.call-start = ((), (), s32[]{:S(2)}) async-start(), calls=%async_computation.2 | async-start | bytes 9437184 | tf_op jit(solution)/shard_map/reduce_scatter | solution.py:22
  125.8 0.7 copy-start.1
  125.8 0.7 copy-start.2
  139.2 3.6 %copy-start = (bf16[512,4096]{1,0:T(8,128)(2,1)S(1)}, bf16[512,4096]{1,0:T(8,128)(2,1)}, u32[]{:S(2)}) copy-start(bf16[512,4096]{1,0:T(8,128)(2,1)} %param.5) | copy-start | bytes 12582916
Sparse Core Ops, SparseCore 0:
  10.5 104.9 all-gather.1
  125.9 52.6 reduce-scatter.1
where the time goes:
time: 234 us
  waiting for transfers between devices  108 us (46%)
  blocking collectives  85.8 us (37%)
  matrix products  18.4 us (8%)
  between operations  14.1 us (6%)
  other arithmetic  5.2 us (2%)
    all_gather x1, waiting for transfers between devices, on_device(): whole = lax.all_gather(embeddings, 'cent', axis=1, tiled=True)  107 us
    pmax x1, blocking collectives, on_device(): top_score = lax.pmax(jnp.max(score, axis=1), 'cent')  73.4 us
    psum x1, blocking collectives, on_device(): counts = lax.psum(jnp.sum(match, axis=0, dtype=jnp.float32), 'dp')  12.4 us
    dot_general x1, matrix products, on_device(): lax.dot_general(whole, onehot, (((0,), (0,)), ((), ())), preferred_elemen...  10.4 us
    dot_general x1, matrix products, on_device(): lax.dot_general(whole, centroids, (((1,), (1,)), ((), ())), preferred_ele...  8.07 us
  transfers between devices with their start and end apart: 2, of which 1 were waited for; matrix products, arithmetic and copies ran while one was open for 5% of the time, Pallas kernels for 0%

commit v1 on v0

v1 whole, which is shorter than its diff:
```python
import functools

import jax
import jax.numpy as jnp
from jax import lax
from jax.experimental import pallas as pl
from jax.experimental.pallas import tpu as pltpu
from jax.sharding import PartitionSpec as P

NX, NY, NZ = 4, 4, 8
ROWS = 1024
WIDTH = 128
CENT = 512
FEAT = 4096
CAP = 64
SLICE = 512
HEAD = 448
HALF = 256
QUART = CENT // NX
PIECES = 4
PIECE = QUART // PIECES
SLOT_Y = (0, 3, 1, 2)
F32, BF16 = jnp.float32, jnp.bfloat16
NT = (((1,), (1,)), ((), ()))
NN = (((1,), (0,)), ((), ()))


def dot(a, b, dims):
    return lax.dot_general(a, b, dims, preferred_element_type=F32)


def kernel(
    emb, cen, asg, prior, top, num, den,
    e, c, acc, cs, sel, rows, ids_out, ids_in, asg_in, pick, hn, best, best_leaf, best_z, best_y,
    s_za, r_za, s_zb, r_zb, s_ya, r_ya, s_yb, r_yb, s_ext, r_ext, s_la, r_la, s_lb, r_lb,
    s_cc, r_cc, s_x1, r_x1, s_x2, r_x2, s_sel, r_sel, s_ids, r_ids, s_bl, r_bl, s_bz, r_bz, s_by, r_by,
    s_asg, r_asg, l_own, l_c, l_cs,
):
    dp, ce = lax.axis_index("dp"), lax.axis_index("cent")
    x, q, y, z = dp // 2, dp % 2, ce // NZ, ce % NZ
    h = y // 2
    pair = ((y + 1) // 2) % 2
    other_y, across = y + 1 - 2 * (y % 2), 3 - y
    group = 2 * x + h
    is_hub = q == h

    def at(x_, q_, y_, z_):
        return (2 * x_ + q_, NZ * y_ + z_)

    def send(src, dst, ss, rs, dev):
        return pltpu.make_async_remote_copy(
            src_ref=src, dst_ref=dst, send_sem=ss, recv_sem=rs,
            device_id=dev, device_id_type=pl.DeviceIdType.MESH,
        )

    def got(dst, ss, rs):
        send(dst, dst, ss, rs, (dp, ce)).wait_recv()

    def slot(b, k):
        p = pair if b == 0 else 1 - pair
        return 2 * p + (h if k == 0 else 1 - h)

    def zof(d, s):
        return (z + NZ - s) % NZ if d == 0 else (z + s) % NZ

    def za_rows(d, s):
        return pl.ds(0, HEAD) if s < 4 else pl.ds(d * (HEAD // 2), HEAD // 2)

    def zb_rows(d, s):
        n = ROWS - HEAD
        return pl.ds(HEAD, n) if s < 4 else pl.ds(HEAD + d * (n // 2), n // 2)

    def za(d, s, b, k):
        where = e.at[zof(d, s - 1), slot(b, k), za_rows(d, s)]
        src = emb.at[za_rows(d, s)] if (s, b, k) == (1, 0, 0) else where
        return send(src, where, s_za.at[d, s - 1, b, k], r_za.at[d, s - 1, b, k], at(x, q, y, zof(1 - d, 1)))

    def za_got(d, s, b, k):
        got(e.at[zof(d, s), slot(b, k), za_rows(d, s)], s_za.at[d, s - 1, b, k], r_za.at[d, s - 1, b, k])

    def zb(d, s, k):
        where = e.at[zof(d, s - 1), slot(0, k), zb_rows(d, s)]
        src = emb.at[zb_rows(d, s)] if (s, k) == (1, 0) else where
        return send(src, where, s_zb.at[d, s - 1, k], r_zb.at[d, s - 1, k], at(x, q, y, zof(1 - d, 1)))

    def zb_got(d, s, k):
        got(e.at[zof(d, s), slot(0, k), zb_rows(d, s)], s_zb.at[d, s - 1, k], r_zb.at[d, s - 1, k])

    def ya(k):
        where = e.at[z, slot(0, k), pl.ds(0, HEAD)]
        src = emb.at[pl.ds(0, HEAD)] if k == 0 else where
        return send(src, where, s_ya.at[k], r_ya.at[k], at(x, q, other_y, z))

    def ya_got(k):
        got(e.at[z, slot(1, k), pl.ds(0, HEAD)], s_ya.at[k], r_ya.at[k])

    def yb(d, s, k):
        where = e.at[zof(d, s), slot(0, k), zb_rows(d, s)]
        src = emb.at[zb_rows(d, s)] if (s, k) == (0, 0) else where
        return send(src, where, s_yb.at[d, s, k], r_yb.at[d, s, k], at(x, q, other_y, z))

    def yb_got(d, s, k):
        got(e.at[zof(d, s), slot(1, k), zb_rows(d, s)], s_yb.at[d, s, k], r_yb.at[d, s, k])

    def la(d, s):
        where = e.at[zof(d, s), :, pl.ds(0, HEAD)]
        return send(where, where, s_la.at[d, s], r_la.at[d, s], at(x, 1 - q, y, z))

    def lb(d, s):
        where = e.at[zof(d, s), :, pl.ds(HEAD, ROWS - HEAD)]
        return send(where, where, s_lb.at[d, s], r_lb.at[d, s], at(x, 1 - q, y, z))

    def dirs(s):
        return (0,) if s in (0, 4) else (0, 1)

    def sel_send(d, s, k, act, y_to):
        zo = zof(d, s)
        to = at(SLOT_Y[k], zo // 4, y_to, z)
        same = (to[0] == dp) & (to[1] == ce)
        src, dst = sel.at[zo, k], rows.at[group, zo % 4]

        @pl.when(jnp.logical_not(same))
        def _():
            cp = send(src, dst, s_sel.at[d, s, k], r_sel.at[group, zo % 4], to)
            cp.start() if act == "start" else cp.wait_send()

        if act == "start":

            @pl.when(same)
            def _():
                pltpu.make_async_copy(src, dst, r_sel.at[group, zo % 4]).start()

    def ids_send(n, act, y_to):
        to = at(n // 2, n % 2, y_to, z)
        same = (to[0] == dp) & (to[1] == ce)

        @pl.when(jnp.logical_not(same))
        def _():
            cp = send(ids_out, ids_in.at[group], s_ids.at[n], r_ids.at[group], to)
            cp.start() if act == "start" else cp.wait_send()

        if act == "start":

            @pl.when(same)
            def _():
                pltpu.make_async_copy(ids_out, ids_in.at[group], r_ids.at[group]).start()

    def choose(a_ref, y_to):
        a = a_ref[...] - CENT * (NZ * y_to + z)
        mask = (a >= 0) & (a < CENT)
        m = jnp.where(mask, 1.0, 0.0).astype(F32)
        mb = m.astype(BF16)
        i0 = lax.broadcasted_iota(jnp.int32, (128, 128), 0)
        i1 = lax.broadcasted_iota(jnp.int32, (128, 128), 1)
        before = dot(mb, jnp.where(i0 < i1, 1.0, 0.0).astype(BF16), NN)
        total = dot(mb, jnp.ones((128, 128), BF16), NN)
        v = jnp.where(mask, a + 1, 0)
        high, low = (v // 32).astype(F32), (v % 32).astype(F32)
        first = lax.broadcasted_iota(jnp.int32, (8, 128), 0) == 0
        rank_of = lax.broadcasted_iota(jnp.int32, (128, 128), 0).astype(F32)
        off = (CAP * h).astype(F32)
        run = jnp.zeros((1, 128), F32)
        ids = jnp.zeros((8, 128), F32)
        for i in range(8):
            here = m[i : i + 1] > 0.5
            rank = before[i : i + 1] + run
            run = run + total[i : i + 1]
            one = jnp.where((rank == rank_of) & here, 1.0, 0.0).astype(BF16)
            pick[:, 128 * i : 128 * (i + 1)] = one[:CAP]
            put = jnp.where((rank + off == rank_of) & here, 1.0, 0.0).astype(BF16)
            vals = jnp.where(first, high[i : i + 1], low[i : i + 1]).astype(BF16)
            ids = ids + dot(vals, put, NT)
        ids_out[...] = jnp.broadcast_to(32.0 * ids[0:1] + ids[1:2] - 1.0, (8, 128))

    def norms():
        @pl.loop(0, CENT // 128)
        def _(i):
            part = jnp.zeros((128, 128), F32)
            r = pl.ds(pl.multiple_of(i * 128, 128), 128)
            for k in range(FEAT // 128):
                v = c[r, k * 128 : (k + 1) * 128].astype(F32)
                part = part + v * v
            hn[r, :] = 0.5 * jnp.sum(part, axis=1, keepdims=True)

    def work(s, y_to):
        n = len(dirs(s))

        @pl.loop(0, n * (ROWS // HALF))
        def _(t):
            i = t % (ROWS // HALF)
            d = t // (ROWS // HALF)
            zo = (z + NZ - s + 2 * s * d) % NZ
            r = pl.ds(pl.multiple_of(i * HALF, HALF), HALF)
            left = jnp.concatenate(
                [c[:, pl.ds(pl.multiple_of(yy * 1024 + zo * 128, 128), 128)] for yy in SLOT_Y], axis=1
            )
            right = jnp.concatenate([e[zo, k, r, :] for k in range(4)], axis=1)
            got_ = dot(left, right, NT)
            if s == 0:
                acc[i] = got_
            else:
                acc[i] += got_

        for d in dirs(s):
            zo = zof(d, s)
            for k in range(4):
                sel[zo, k] = dot(pick[...], e[zo, k], NN).astype(BF16)
                sel_send(d, s, k, "start", y_to)

    def top_rows():
        for i in range(ROWS // HALF):
            m = jnp.max(acc[i] - hn[...], axis=0, keepdims=True)
            best[2 * i : 2 * i + 1, :] = m[:, :128]
            best[2 * i + 1 : 2 * i + 2, :] = m[:, 128:]

    barrier = pltpu.get_barrier_semaphore()
    peers = [((dp + k) % 8, NZ * yy + z) for k in range(8) for yy in (y, across) if not (k == 0 and yy is y)]
    peers += [(dp, NZ * y + (z + k) % NZ) for k in range(1, NZ)]
    peers += [(dp, NZ * other_y + z), (dp, NZ * (3 - other_y) + z)]
    for to in peers:
        pl.semaphore_signal(barrier, inc=1, device_id=to, device_id_type=pl.DeviceIdType.MESH)
    pl.semaphore_wait(barrier, len(peers))

    own_slice = pltpu.make_async_copy(cen.at[:, pl.ds(pl.multiple_of(dp * SLICE, SLICE), SLICE)], cs, l_cs)

    def tell(act):
        for yy in range(NY):

            @pl.when(yy != y)
            def _():
                cp = send(best_y.at[y % 2], best_y.at[y % 2], s_by.at[yy], r_by.at[y % 2], at(x, q, yy, z))
                cp.start() if act == "start" else cp.wait_send()

    @pl.when(is_hub)
    def _():
        own = pltpu.make_async_copy(emb, e.at[z, slot(0, 0)], l_own)
        all_c = pltpu.make_async_copy(cen, c, l_c)
        give_asg = send(asg, asg_in, s_asg, r_asg, at(x, 1 - q, y, z))
        ya(0).start()
        for d in (0, 1):
            zb(d, 1, 0).start()
        for d in (0, 1):
            za(d, 1, 0, 0).start()
        yb(0, 0, 0).start()
        give_asg.start()
        own.start()
        all_c.start()
        own_slice.start()
        choose(asg, y)
        for n in range(8):
            ids_send(n, "start", y)
        got(e.at[z, slot(0, 1), pl.ds(0, HEAD)], s_ext.at[0], r_ext.at[0])
        ya(1).start()
        for d in (0, 1):
            za(d, 1, 0, 1).start()
        ya_got(0)
        for d in (0, 1):
            za(d, 1, 1, 0).start()
        got(e.at[z, slot(0, 1), pl.ds(HEAD, ROWS - HEAD)], s_ext.at[1], r_ext.at[1])
        for d in (0, 1):
            zb(d, 1, 1).start()
        yb(0, 0, 1).start()
        ya_got(1)
        for d in (0, 1):
            za(d, 1, 1, 1).start()
        own.wait()
        la(0, 0).start()
        all_c.wait()
        norms()
        for s in range(1, 5):
            for k in (0, 1):
                for d in (0, 1):
                    zb_got(d, s, k)
                    if s < 4:
                        zb(d, s + 1, k).start()
                    yb(d, s, k).start()
            for b, k in ((0, 0), (0, 1), (1, 0), (1, 1)):
                for d in (0, 1):
                    za_got(d, s, b, k)
                    if s < 4:
                        za(d, s + 1, b, k).start()
            for d in dirs(s):
                la(d, s).start()
            for d in dirs(s - 1):
                for k in (0, 1):
                    yb_got(d, s - 1, k)
                lb(d, s - 1).start()
            work(s - 1, y)
        for d in (0, 1):
            for k in (0, 1):
                yb_got(d, 4, k)
        lb(0, 4).start()
        work(4, y)
        top_rows()
        got(best_leaf, s_bl, r_bl)
        best_z[z] = jnp.maximum(best[...], best_leaf[...])
        for k in range(1, NZ):
            send(best_z.at[z], best_z.at[z], s_bz.at[k], r_bz.at[k], at(x, q, y, (z + k) % NZ)).start()

    @pl.when(jnp.logical_not(is_hub))
    def _():
        def ext(n):
            r = pl.ds(0, HEAD) if n == 0 else pl.ds(HEAD, ROWS - HEAD)
            return send(emb.at[r], e.at[z, slot(0, 0), r], s_ext.at[n], r_ext.at[n], at(x, q, across, z))

        def part(n, k):
            return pl.ds(pl.multiple_of(((x + n) % NX) * QUART + k * PIECE, PIECE), PIECE)

        def cross(k):
            return send(cen.at[part(0, k)], c.at[part(0, k)], s_cc.at[k], r_cc.at[k], at(x, 1 - q, across, z))

        def near(d, k):
            to = at((x + 1 + 2 * d) % NX, q, y, z)
            return send(c.at[part(0, k)], c.at[part(0, k)], s_x1.at[d, k], r_x1.at[d, k], to)

        def far(k):
            d = k // 2
            to = at((x + 1 + 2 * d) % NX, q, y, z)
            which = part(3 - 2 * d, k)
            return send(c.at[which], c.at[which], s_x2.at[k], r_x2.at[k], to)

        ext(0).start()
        ext(1).start()
        own_slice.start()
        for n in (0, 1):
            ext(n).wait_send()
        for k in range(PIECES):
            cross(k).start()
        got(asg_in, s_asg, r_asg)
        choose(asg_in, across)
        for n in range(8):
            ids_send(n, "start", across)
        for k in range(PIECES):
            got(c.at[part(0, k)], s_cc.at[k], r_cc.at[k])
            for d in (0, 1):
                near(d, k).start()
            if k:
                for d in (0, 1):
                    got(c.at[part(3 - 2 * d, k - 1)], s_x1.at[d, k - 1], r_x1.at[d, k - 1])
                far(k - 1).start()
        for d in (0, 1):
            got(c.at[part(3 - 2 * d, PIECES - 1)], s_x1.at[d, PIECES - 1], r_x1.at[d, PIECES - 1])
        far(PIECES - 1).start()
        for k in range(PIECES):
            got(c.at[part(2, k)], s_x2.at[k], r_x2.at[k])
        norms()
        for s in range(5):
            for d in dirs(s):
                got(e.at[zof(d, s), :, pl.ds(0, HEAD)], s_la.at[d, s], r_la.at[d, s])
                got(e.at[zof(d, s), :, pl.ds(HEAD, ROWS - HEAD)], s_lb.at[d, s], r_lb.at[d, s])
            work(s, across)
        top_rows()
        give = send(best, best_leaf, s_bl, r_bl, at(x, 1 - q, y, z))
        give.start()
        for n in (0, 1):
            pass
        for k in range(PIECES):
            cross(k).wait_send()
            far(k).wait_send()
            for d in (0, 1):
                near(d, k).wait_send()
        for n in range(8):
            ids_send(n, "wait", across)
        for s in range(5):
            for d in dirs(s):
                for k in range(4):
                    sel_send(d, s, k, "wait", across)
        give.wait_send()

    own_slice.wait()
    pr = prior[...].astype(F32)
    for n in range(8):
        got(ids_in.at[n], s_ids.at[n], r_ids.at[n])
    k_of = lax.broadcasted_iota(jnp.int32, (CENT, 128), 0).astype(F32)
    hot = jnp.concatenate(
        [
            jnp.where(jnp.maximum(ids_in[2 * n, 0:1], ids_in[2 * n + 1, 0:1]) == k_of, 1.0, 0.0).astype(BF16)
            for n in range(4)
        ],
        axis=1,
    )
    counts = dot(jnp.ones((8, SLICE), BF16), hot, NT)
    den[...] = jnp.broadcast_to(pr + counts[0:1], (8, CENT))
    for n in range(8):
        for k in range(4):
            got(rows.at[n, k], s_sel.at[0, 0, 0], r_sel.at[n, k])
    for k in range(4):
        f = slice(k * 128, (k + 1) * 128)
        taken = jnp.concatenate([rows[n, k] for n in range(8)], axis=0)
        num[f, :] = pr * cs[:, f].astype(F32).T + dot(taken.T, hot, NT)

    @pl.when(is_hub)
    def _():
        for k in range(1, NZ):
            zs = (z + NZ - k) % NZ
            got(best_z.at[zs], s_bz.at[k], r_bz.at[k])
        m = best_z[0]
        for k in range(1, NZ):
            m = jnp.maximum(m, best_z[k])
        best_y[y % 2] = m
        tell("start")
        got(best_y.at[1 - y % 2], s_by.at[0], r_by.at[1 - y % 2])
        for s in range(1, 5):
            for d in (0, 1):
                for k in (0, 1):
                    zb(d, s, k).wait_send()
                    yb(d, s, k).wait_send()
                    for b in (0, 1):
                        za(d, s, b, k).wait_send()
        for k in (0, 1):
            ya(k).wait_send()
            yb(0, 0, k).wait_send()
        for s in range(5):
            for d in dirs(s):
                la(d, s).wait_send()
                lb(d, s).wait_send()
                for k in range(4):
                    sel_send(d, s, k, "wait", y)
        for n in range(8):
            ids_send(n, "wait", y)
        send(asg, asg_in, s_asg, r_asg, at(x, 1 - q, y, z)).wait_send()
        for k in range(1, NZ):
            send(best_z.at[z], best_z.at[z], s_bz.at[k], r_bz.at[k], at(x, q, y, (z + k) % NZ)).wait_send()
        tell("wait")

    @pl.when(jnp.logical_not(is_hub))
    def _():
        for n in (0, 1):
            got(best_y.at[n], s_by.at[n], r_by.at[n])

    top[...] = jnp.maximum(best_y[0], best_y[1])


def on_device(embeddings, centroids, assignment, prior_counts):
    dma = pltpu.SemaphoreType.DMA
    both = lambda *shape: [dma(shape), dma(shape)]
    vmem, hbm = pl.BlockSpec(memory_space=pltpu.VMEM), pl.BlockSpec(memory_space=pl.ANY)
    top, num, den = pl.pallas_call(
        kernel,
        out_shape=[
            jax.ShapeDtypeStruct((8, 128), F32),
            jax.ShapeDtypeStruct((SLICE, CENT), F32),
            jax.ShapeDtypeStruct((8, CENT), F32),
        ],
        in_specs=[hbm, hbm, vmem, vmem],
        out_specs=[vmem, vmem, vmem],
        scratch_shapes=[
            pltpu.VMEM((NZ, 4, ROWS, WIDTH), BF16),
            pltpu.VMEM((CENT, FEAT), BF16),
            pltpu.VMEM((ROWS // HALF, CENT, HALF), F32),
            pltpu.VMEM((CENT, SLICE), BF16),
            pltpu.VMEM((NZ, 4, CAP, WIDTH), BF16),
            pltpu.VMEM((8, 4, CAP, WIDTH), BF16),
            pltpu.VMEM((8, 128), F32),
            pltpu.VMEM((8, 8, 128), F32),
            pltpu.VMEM((8, 128), jnp.int32),
            pltpu.VMEM((CAP, ROWS), BF16),
            pltpu.VMEM((CENT, 1), F32),
            pltpu.VMEM((8, 128), F32),
            pltpu.VMEM((8, 128), F32),
            pltpu.VMEM((NZ, 8, 128), F32),
            pltpu.VMEM((2, 8, 128), F32),
            *both(2, 4, 2, 2),
            *both(2, 4, 2),
            *both(2),
            *both(2, 5, 2),
            *both(2),
            *both(2, 5),
            *both(2, 5),
            *both(PIECES),
            *both(2, PIECES),
            *both(PIECES),
            dma((2, 5, 4)), dma((8, 4)),
            *both(8),
            dma(()), dma(()),
            *both(NZ),
            dma((4,)), dma((2,)),
            dma(()), dma(()),
            dma(()), dma(()), dma(()),
        ],
        compiler_params=pltpu.CompilerParams(
            collective_id=0, has_side_effects=True, vmem_limit_bytes=40 * 2**20
        ),
        name="score_and_update",
    )(embeddings, centroids, assignment.reshape(8, 128), prior_counts.reshape(1, CENT))
    return top.reshape(ROWS), num / den[0:1]


def solution(mesh):
    placed = (P("dp", "cent"), P("cent", None), P("dp"), P("cent"))
    return jax.shard_map(
        on_device, mesh=mesh, in_specs=placed, out_specs=(P("dp"), P("dp", "cent")), check_vma=False
    )
```

time: 234 us -> 82.2 us (0.35)
  the two profiles are of different devices: /device:TPU:0 before, /device:TPU:1 now
where the time goes in v1:
time: 82.2 us; the launch traced here: 82 us
  Pallas kernels  75.1 us (91%)
  local copies, waits for them, and re-layouts  5.09 us (6%)
  other arithmetic  1.12 us (1%)
    pallas_call x1, Pallas kernels, on_device(): pl.pallas_call(kernel, out_shape=[jax.ShapeDtypeStruct((8, 128), F32), ja...  75.1 us
    unnamed x9, local copies, waits for them, and re-layouts  5.09 us

profile of v1, /device:TPU:1, one launch (start us, length us, event | category | flops | bytes accessed | tf_op | source)
XLA Modules:
  0.0 82.0 jit_solution(757669169566243862)
XLA Ops:
  0.6 0.0 copy-start
  0.6 2.2 %copy-done = bf16[512,4096]{1,0:T(8,128)(2,1)S(1)} copy-done((bf16[512,4096]{1,0:T(8,128)(2,1)S(1)}, bf16[512,4096]{1,0:T(8,128)(2,1)}, u32[]{:S(2)}) %copy-start) | copy-done | bytes 4194328
  2.8 0.0 copy-start.1
  2.8 0.9 %copy-done.1 = bf16[1024,128]{1,0:T(8,128)(2,1)S(1)} copy-done((bf16[1024,128]{1,0:T(8,128)(2,1)S(1)}, bf16[1024,128]{1,0:T(8,128)(2,1)}, u32[]{:S(2)}) %copy-start.1) | copy-done | bytes 262168
  3.8 0.0 copy-start.2
  3.8 0.7 copy-done.2
  4.5 0.0 copy-start.3
  4.5 0.7 copy-done.3
  5.1 75.1 %score_and_update.1 = (f32[8,128]{1,0:T(8,128)S(1)}, f32[512,512]{1,0:T(8,128)S(1)}, f32[8,512]{1,0:T(8,128)S(1)}) custom-call(bf16[1024,128]{1,0:T(8,128)(2,1)S(1)} %copy-done.1, bf16[512,4096]{1,0:T(8,128)(2,1)S(1)} %copy-done, s32[8,128]{1,0:T(8,128)S(1)} %bitcast.4, s32[1,512]{1,0:T(1,128)S(1)} %bitcast.6), custom_call_target="tpu_custom_call" | custom-call | tf_op jit(solution)/shard_map/score_and_update/pallas_call | solution.py:438
  80.3 1.1 %broadcast_divide_fusion = f32[512,512]{1,0:T(8,128)} fusion(f32[512,512]{1,0:T(8,128)S(1)} %get-tuple-element.6, f32[512]{0:T(512)S(1)} %bitcast.7), kind=kLoop, calls=%fused_computation | loop fusion | flops 262144 | bytes 2099200 | tf_op jit(solution)/shard_map/div | solution.py:486
  81.4 0.6 copy.7
  (1 shorter events, 0.0 us)
Async XLA Ops:
  0.6 2.2 %copy-start = (bf16[512,4096]{1,0:T(8,128)(2,1)S(1)}, bf16[512,4096]{1,0:T(8,128)(2,1)}, u32[]{:S(2)}) copy-start(bf16[512,4096]{1,0:T(8,128)(2,1)} %cen.1) | copy-start | bytes 12582916
  2.8 0.9 %copy-start.1 = (bf16[1024,128]{1,0:T(8,128)(2,1)S(1)}, bf16[1024,128]{1,0:T(8,128)(2,1)}, u32[]{:S(2)}) copy-start(bf16[1024,128]{1,0:T(8,128)(2,1)} %emb.1) | copy-start | bytes 786436
  3.8 0.7 copy-start.2
  4.5 0.7 copy-start.3

commit v2 on v1

--- a/solution.py
+++ b/solution.py
@@ -15,9 +15,8 @@
 CAP = 64
 SLICE = 512
 HEAD = 448
-HALF = 256
 QUART = CENT // NX
-PIECES = 4
+PIECES = 8
 PIECE = QUART // PIECES
 SLOT_Y = (0, 3, 1, 2)
 F32, BF16 = jnp.float32, jnp.bfloat16
@@ -30,11 +29,11 @@
 
 
 def kernel(
-    emb, cen, asg, prior, top, num, den,
-    e, c, acc, cs, sel, rows, ids_out, ids_in, asg_in, pick, hn, best, best_leaf, best_z, best_y,
+    emb, cen, asg_hbm, prior_hbm, top, num, den,
+    e, c, acc, cs, sel, rows, ids_out, ids_in, asg, asg_in, prior, pick, hn, best, best_leaf, best_z, best_y,
     s_za, r_za, s_zb, r_zb, s_ya, r_ya, s_yb, r_yb, s_ext, r_ext, s_la, r_la, s_lb, r_lb,
     s_cc, r_cc, s_x1, r_x1, s_x2, r_x2, s_sel, r_sel, s_ids, r_ids, s_bl, r_bl, s_bz, r_bz, s_by, r_by,
-    s_asg, r_asg, l_own, l_c, l_cs,
+    s_asg, r_asg, l_own, l_c, l_cs, l_asg, l_prior,
 ):
     dp, ce = lax.axis_index("dp"), lax.axis_index("cent")
     x, q, y, z = dp // 2, dp % 2, ce // NZ, ce % NZ
@@ -113,15 +112,22 @@
     def dirs(s):
         return (0,) if s in (0, 4) else (0, 1)
 
-    def sel_send(d, s, k, act, y_to):
-        zo = zof(d, s)
+    def blocks(s):
+        return (0, 1) if s == 0 else (2 * s - 1, min(2 * s + 1, NZ))
+
+    def zon(n):
+        far = (n + 1) // 2
+        return (z + NZ + far * (1 - 2 * (n % 2))) % NZ
+
+    def sel_send(n, k, act, y_to):
+        zo = zon(n)
         to = at(SLOT_Y[k], zo // 4, y_to, z)
         same = (to[0] == dp) & (to[1] == ce)
         src, dst = sel.at[zo, k], rows.at[group, zo % 4]
 
         @pl.when(jnp.logical_not(same))
         def _():
-            cp = send(src, dst, s_sel.at[d, s, k], r_sel.at[group, zo % 4], to)
+            cp = send(src, dst, s_sel.at[n, k], r_sel.at[group, zo % 4], to)
             cp.start() if act == "start" else cp.wait_send()
 
         if act == "start":
@@ -172,48 +178,52 @@
             ids = ids + dot(vals, put, NT)
         ids_out[...] = jnp.broadcast_to(32.0 * ids[0:1] + ids[1:2] - 1.0, (8, 128))
 
-    def norms():
-        @pl.loop(0, CENT // 128)
+    def norms(first, count):
+        @pl.loop(0, count)
         def _(i):
             part = jnp.zeros((128, 128), F32)
-            r = pl.ds(pl.multiple_of(i * 128, 128), 128)
+            r = pl.ds(pl.multiple_of((first + i) % NX * 128, 128), 128)
             for k in range(FEAT // 128):
                 v = c[r, k * 128 : (k + 1) * 128].astype(F32)
                 part = part + v * v
             hn[r, :] = 0.5 * jnp.sum(part, axis=1, keepdims=True)
 
-    def work(s, y_to):
-        n = len(dirs(s))
-
-        @pl.loop(0, n * (ROWS // HALF))
-        def _(t):
-            i = t % (ROWS // HALF)
-            d = t // (ROWS // HALF)
-            zo = (z + NZ - s + 2 * s * d) % NZ
-            r = pl.ds(pl.multiple_of(i * HALF, HALF), HALF)
+    def choose_rows(lo, hi, y_to):
+        @pl.loop(lo, hi)
+        def _(n):
+            zo = zon(n)
+            for k in range(4):
+                sel[zo, k] = dot(pick[...], e[zo, k], NN).astype(BF16)
+                sel_send(n, k, "start", y_to)
+
+    def score(lo, hi):
+        def one(n):
+            zo = zon(n)
             left = jnp.concatenate(
                 [c[:, pl.ds(pl.multiple_of(yy * 1024 + zo * 128, 128), 128)] for yy in SLOT_Y], axis=1
             )
-            right = jnp.concatenate([e[zo, k, r, :] for k in range(4)], axis=1)
-            got_ = dot(left, right, NT)
-            if s == 0:
-                acc[i] = got_
-            else:
-                acc[i] += got_
-
-        for d in dirs(s):
-            zo = zof(d, s)
-            for k in range(4):
-                sel[zo, k] = dot(pick[...], e[zo, k], NN).astype(BF16)
-                sel_send(d, s, k, "start", y_to)
+            return dot(left, jnp.concatenate([e[zo, k] for k in range(4)], axis=1), NT)
+
+        if lo == 0:
+            acc[...] = one(0)
+        else:
+
+            @pl.loop(lo, hi)
+            def _(n):
+                acc[...] += one(n)
 
     def top_rows():
-        for i in range(ROWS // HALF):
-            m = jnp.max(acc[i] - hn[...], axis=0, keepdims=True)
-            best[2 * i : 2 * i + 1, :] = m[:, :128]
-            best[2 * i + 1 : 2 * i + 2, :] = m[:, 128:]
+        m = jnp.max(acc[...] - hn[...], axis=0, keepdims=True)
+        for i in range(8):
+            best[i : i + 1, :] = m[:, 128 * i : 128 * (i + 1)]
 
     barrier = pltpu.get_barrier_semaphore()
+    own_slice = pltpu.make_async_copy(cen.at[:, pl.ds(pl.multiple_of(dp * SLICE, SLICE), SLICE)], cs, l_cs)
+    own_asg = pltpu.make_async_copy(asg_hbm, asg, l_asg)
+    own_prior = pltpu.make_async_copy(prior_hbm, prior, l_prior)
+    own_asg.start()
+    own_prior.start()
+    own_slice.start()
     peers = [((dp + k) % 8, NZ * yy + z) for k in range(8) for yy in (y, across) if not (k == 0 and yy is y)]
     peers += [(dp, NZ * y + (z + k) % NZ) for k in range(1, NZ)]
     peers += [(dp, NZ * other_y + z), (dp, NZ * (3 - other_y) + z)]
@@ -221,8 +231,6 @@
         pl.semaphore_signal(barrier, inc=1, device_id=to, device_id_type=pl.DeviceIdType.MESH)
     pl.semaphore_wait(barrier, len(peers))
 
-    own_slice = pltpu.make_async_copy(cen.at[:, pl.ds(pl.multiple_of(dp * SLICE, SLICE), SLICE)], cs, l_cs)
-
     def tell(act):
         for yy in range(NY):
 
@@ -236,19 +244,16 @@
         own = pltpu.make_async_copy(emb, e.at[z, slot(0, 0)], l_own)
         all_c = pltpu.make_async_copy(cen, c, l_c)
         give_asg = send(asg, asg_in, s_asg, r_asg, at(x, 1 - q, y, z))
+        for d in (0, 1):
+            zb(d, 1, 0).start()
+        for d in (0, 1):
+            za(d, 1, 0, 0).start()
         ya(0).start()
-        for d in (0, 1):
-            zb(d, 1, 0).start()
-        for d in (0, 1):
-            za(d, 1, 0, 0).start()
         yb(0, 0, 0).start()
-        give_asg.start()
         own.start()
         all_c.start()
-        own_slice.start()
-        choose(asg, y)
-        for n in range(8):
-            ids_send(n, "start", y)
+        own_asg.wait()
+        give_asg.start()
         got(e.at[z, slot(0, 1), pl.ds(0, HEAD)], s_ext.at[0], r_ext.at[0])
         ya(1).start()
         for d in (0, 1):
@@ -265,8 +270,6 @@
             za(d, 1, 1, 1).start()
         own.wait()
         la(0, 0).start()
-        all_c.wait()
-        norms()
         for s in range(1, 5):
             for k in (0, 1):
                 for d in (0, 1):
@@ -274,6 +277,10 @@
                     if s < 4:
                         zb(d, s + 1, k).start()
                     yb(d, s, k).start()
+            if s == 1:
+                choose(asg, y)
+                for n in range(8):
+                    ids_send(n, "start", y)
             for b, k in ((0, 0), (0, 1), (1, 0), (1, 1)):
                 for d in (0, 1):
                     za_got(d, s, b, k)
@@ -285,12 +292,17 @@
                 for k in (0, 1):
                     yb_got(d, s - 1, k)
                 lb(d, s - 1).start()
-            work(s - 1, y)
+            if s == 1:
+                all_c.wait()
+                norms(0, NX)
+            choose_rows(*blocks(s - 1), y)
+            score(*blocks(s - 1))
         for d in (0, 1):
             for k in (0, 1):
                 yb_got(d, 4, k)
         lb(0, 4).start()
-        work(4, y)
+        choose_rows(*blocks(4), y)
+        score(*blocks(4))
         top_rows()
         got(best_leaf, s_bl, r_bl)
         best_z[z] = jnp.maximum(best[...], best_leaf[...])
@@ -314,14 +326,14 @@
             return send(c.at[part(0, k)], c.at[part(0, k)], s_x1.at[d, k], r_x1.at[d, k], to)
 
         def far(k):
-            d = k // 2
+            d = k // (PIECES // 2)
             to = at((x + 1 + 2 * d) % NX, q, y, z)
             which = part(3 - 2 * d, k)
             return send(c.at[which], c.at[which], s_x2.at[k], r_x2.at[k], to)
 
         ext(0).start()
         ext(1).start()
-        own_slice.start()
+        own_asg.wait()
         for n in (0, 1):
             ext(n).wait_send()
         for k in range(PIECES):
@@ -330,30 +342,42 @@
         choose(asg_in, across)
         for n in range(8):
             ids_send(n, "start", across)
+
+        def pass_on(k):
+            for d in (0, 1):
+                got(c.at[part(3 - 2 * d, k)], s_x1.at[d, k], r_x1.at[d, k])
+            far(k).start()
+
+        def arrived(s):
+            for d in dirs(s):
+                got(e.at[zof(d, s), :, pl.ds(0, HEAD)], s_la.at[d, s], r_la.at[d, s])
+                got(e.at[zof(d, s), :, pl.ds(HEAD, ROWS - HEAD)], s_lb.at[d, s], r_lb.at[d, s])
+            choose_rows(*blocks(s), across)
+
         for k in range(PIECES):
             got(c.at[part(0, k)], s_cc.at[k], r_cc.at[k])
             for d in (0, 1):
                 near(d, k).start()
-            if k:
-                for d in (0, 1):
-                    got(c.at[part(3 - 2 * d, k - 1)], s_x1.at[d, k - 1], r_x1.at[d, k - 1])
-                far(k - 1).start()
-        for d in (0, 1):
-            got(c.at[part(3 - 2 * d, PIECES - 1)], s_x1.at[d, PIECES - 1], r_x1.at[d, PIECES - 1])
-        far(PIECES - 1).start()
+            if k > 1:
+                pass_on(k - 2)
+        arrived(0)
+        for k in range(PIECES - 2, PIECES):
+            pass_on(k)
+        norms(x, 2)
+        norms(x + 3, 1)
+        arrived(1)
+        arrived(2)
         for k in range(PIECES):
             got(c.at[part(2, k)], s_x2.at[k], r_x2.at[k])
-        norms()
-        for s in range(5):
-            for d in dirs(s):
-                got(e.at[zof(d, s), :, pl.ds(0, HEAD)], s_la.at[d, s], r_la.at[d, s])
-                got(e.at[zof(d, s), :, pl.ds(HEAD, ROWS - HEAD)], s_lb.at[d, s], r_lb.at[d, s])
-            work(s, across)
+        norms(x + 2, 1)
+        score(0, 1)
+        score(1, 5)
+        for s in (3, 4):
+            arrived(s)
+            score(*blocks(s))
         top_rows()
         give = send(best, best_leaf, s_bl, r_bl, at(x, 1 - q, y, z))
         give.start()
-        for n in (0, 1):
-            pass
         for k in range(PIECES):
             cross(k).wait_send()
             far(k).wait_send()
@@ -361,13 +385,13 @@
                 near(d, k).wait_send()
         for n in range(8):
             ids_send(n, "wait", across)
-        for s in range(5):
-            for d in dirs(s):
-                for k in range(4):
-                    sel_send(d, s, k, "wait", across)
+        for n in range(NZ):
+            for k in range(4):
+                sel_send(n, k, "wait", across)
         give.wait_send()
 
     own_slice.wait()
+    own_prior.wait()
     pr = prior[...].astype(F32)
     for n in range(8):
         got(ids_in.at[n], s_ids.at[n], r_ids.at[n])
@@ -380,10 +404,10 @@
         axis=1,
     )
     counts = dot(jnp.ones((8, SLICE), BF16), hot, NT)
-    den[...] = jnp.broadcast_to(pr + counts[0:1], (8, CENT))
+    den[...] = pr + counts[0:1]
     for n in range(8):
         for k in range(4):
-            got(rows.at[n, k], s_sel.at[0, 0, 0], r_sel.at[n, k])
+            got(rows.at[n, k], s_sel.at[0, 0], r_sel.at[n, k])
     for k in range(4):
         f = slice(k * 128, (k + 1) * 128)
         taken = jnp.concatenate([rows[n, k] for n in range(8)], axis=0)
@@ -414,8 +438,9 @@
             for d in dirs(s):
                 la(d, s).wait_send()
                 lb(d, s).wait_send()
-                for k in range(4):
-                    sel_send(d, s, k, "wait", y)
+        for n in range(NZ):
+            for k in range(4):
+                sel_send(n, k, "wait", y)
         for n in range(8):
             ids_send(n, "wait", y)
         send(asg, asg_in, s_asg, r_asg, at(x, 1 - q, y, z)).wait_send()
@@ -434,26 +459,30 @@
 def on_device(embeddings, centroids, assignment, prior_counts):
     dma = pltpu.SemaphoreType.DMA
     both = lambda *shape: [dma(shape), dma(shape)]
-    vmem, hbm = pl.BlockSpec(memory_space=pltpu.VMEM), pl.BlockSpec(memory_space=pl.ANY)
+    vmem, hbm = pl.BlockSpec(memory_space=pltpu.VMEM), pl.BlockSpec(memory_space=pltpu.HBM)
+    placed = (embeddings, centroids, assignment.reshape(8, 128), prior_counts.reshape(1, CENT))
+    placed = [pltpu.with_memory_space_constraint(v, pltpu.HBM) for v in placed]
     top, num, den = pl.pallas_call(
         kernel,
         out_shape=[
             jax.ShapeDtypeStruct((8, 128), F32),
             jax.ShapeDtypeStruct((SLICE, CENT), F32),
-            jax.ShapeDtypeStruct((8, CENT), F32),
+            jax.ShapeDtypeStruct((1, CENT), F32),
         ],
-        in_specs=[hbm, hbm, vmem, vmem],
+        in_specs=[hbm, hbm, hbm, hbm],
         out_specs=[vmem, vmem, vmem],
         scratch_shapes=[
             pltpu.VMEM((NZ, 4, ROWS, WIDTH), BF16),
             pltpu.VMEM((CENT, FEAT), BF16),
-            pltpu.VMEM((ROWS // HALF, CENT, HALF), F32),
+            pltpu.VMEM((CENT, ROWS), F32),
             pltpu.VMEM((CENT, SLICE), BF16),
             pltpu.VMEM((NZ, 4, CAP, WIDTH), BF16),
             pltpu.VMEM((8, 4, CAP, WIDTH), BF16),
             pltpu.VMEM((8, 128), F32),
             pltpu.VMEM((8, 8, 128), F32),
             pltpu.VMEM((8, 128), jnp.int32),
+            pltpu.VMEM((8, 128), jnp.int32),
+            pltpu.VMEM((1, CENT), jnp.int32),
             pltpu.VMEM((CAP, ROWS), BF16),
             pltpu.VMEM((CENT, 1), F32),
             pltpu.VMEM((8, 128), F32),
@@ -470,20 +499,20 @@
             *both(PIECES),
             *both(2, PIECES),
             *both(PIECES),
-            dma((2, 5, 4)), dma((8, 4)),
+            dma((NZ, 4)), dma((8, 4)),
             *both(8),
             dma(()), dma(()),
             *both(NZ),
             dma((4,)), dma((2,)),
             dma(()), dma(()),
-            dma(()), dma(()), dma(()),
+            *both(), *both(), dma(()),
         ],
         compiler_params=pltpu.CompilerParams(
             collective_id=0, has_side_effects=True, vmem_limit_bytes=40 * 2**20
         ),
         name="score_and_update",
-    )(embeddings, centroids, assignment.reshape(8, 128), prior_counts.reshape(1, CENT))
-    return top.reshape(ROWS), num / den[0:1]
+    )(*placed)
+    return top.reshape(ROWS), num / den
 
 
 def solution(mesh):

time: 82.2 us -> 65.9 us (0.80)
  Pallas kernels: 75.1 us -> 63.2 us
  local copies, waits for them, and re-layouts: 5.09 us -> 0.59 us
    pallas_call x1, Pallas kernels: 75.1 us -> 63.2 us  [on_device(): pl.pallas_call(kernel, out_shape=[jax.ShapeDtypeStruct((8, 128), F32), ja...]
    unnamed x9 -> x1, local copies, waits for them, and re-layouts: 5.09 us -> 0.59 us
where the time goes in v2:
time: 65.9 us; the launch traced here: 65.6 us
  Pallas kernels  63.2 us (96%)
  other arithmetic  1.11 us (2%)
    pallas_call x1, Pallas kernels, on_device(): pl.pallas_call(kernel, out_shape=[jax.ShapeDtypeStruct((8, 128), F32), ja...  63.2 us

profile of v2, /device:TPU:1, one launch (start us, length us, event | category | flops | bytes accessed | tf_op | source)
XLA Modules:
  0.0 65.6 jit_solution(13911180780079522220)
XLA Ops:
  0.6 63.2 %score_and_update.1 = (f32[8,128]{1,0:T(8,128)S(1)}, f32[512,512]{1,0:T(8,128)S(1)}, f32[1,512]{1,0:T(1,128)S(1)}) custom-call(bf16[1024,128]{1,0:T(8,128)(2,1)} %emb.1, bf16[512,4096]{1,0:T(8,128)(2,1)} %cen.1, s32[8,128]{1,0:T(8,128)} %bitcast.6, s32[1,512]{1,0:T(1,128)} %bitcast.7), custom_call_target="tpu_custom_call" | custom-call | tf_op jit(solution)/shard_map/score_and_update/pallas_call | solution.py:465
  63.9 1.1 %broadcast_divide_fusion = f32[512,512]{1,0:T(8,128)} fusion(f32[512,512]{1,0:T(8,128)S(1)} %get-tuple-element.6, f32[512]{0:T(512)S(1)} %bitcast.5), kind=kLoop, calls=%fused_computation | loop fusion | flops 262144 | bytes 2099200 | tf_op jit(solution)/shard_map/div | solution.py:515
  65.0 0.6 copy.7

commit v3 on v2

--- a/solution.py
+++ b/solution.py
@@ -31,8 +31,8 @@
 def kernel(
     emb, cen, asg_hbm, prior_hbm, top, num, den,
     e, c, acc, cs, sel, rows, ids_out, ids_in, asg, asg_in, prior, pick, hn, best, best_leaf, best_z, best_y,
-    s_za, r_za, s_zb, r_zb, s_ya, r_ya, s_yb, r_yb, s_ext, r_ext, s_la, r_la, s_lb, r_lb,
-    s_cc, r_cc, s_x1, r_x1, s_x2, r_x2, s_sel, r_sel, s_ids, r_ids, s_bl, r_bl, s_bz, r_bz, s_by, r_by,
+    s_ring, r_za, r_zb, r_ya, r_yb, s_ext, r_ext, s_l, r_la, r_lb, r_l4,
+    s_c, r_cc, r_x1, r_x2, s_sel, r_sel, s_ids, r_ids, s_bl, r_bl, s_bz, r_bz, s_by, r_by,
     s_asg, r_asg, l_own, l_c, l_cs, l_asg, l_prior,
 ):
     dp, ce = lax.axis_index("dp"), lax.axis_index("cent")
@@ -52,8 +52,11 @@
             device_id=dev, device_id_type=pl.DeviceIdType.MESH,
         )
 
-    def got(dst, ss, rs):
-        send(dst, dst, ss, rs, (dp, ce)).wait_recv()
+    def got(dst, rs):
+        send(dst, dst, s_ring, rs, (dp, ce)).wait_recv()
+
+    def sent(src, ss):
+        send(src, src, ss, r_asg, (dp, ce)).wait_send()
 
     def slot(b, k):
         p = pair if b == 0 else 1 - pair
@@ -72,42 +75,50 @@
     def za(d, s, b, k):
         where = e.at[zof(d, s - 1), slot(b, k), za_rows(d, s)]
         src = emb.at[za_rows(d, s)] if (s, b, k) == (1, 0, 0) else where
-        return send(src, where, s_za.at[d, s - 1, b, k], r_za.at[d, s - 1, b, k], at(x, q, y, zof(1 - d, 1)))
+        return send(src, where, s_ring, r_za.at[d, s - 1, b, k], at(x, q, y, zof(1 - d, 1)))
 
     def za_got(d, s, b, k):
-        got(e.at[zof(d, s), slot(b, k), za_rows(d, s)], s_za.at[d, s - 1, b, k], r_za.at[d, s - 1, b, k])
+        got(e.at[zof(d, s), slot(b, k), za_rows(d, s)], r_za.at[d, s - 1, b, k])
 
     def zb(d, s, k):
         where = e.at[zof(d, s - 1), slot(0, k), zb_rows(d, s)]
         src = emb.at[zb_rows(d, s)] if (s, k) == (1, 0) else where
-        return send(src, where, s_zb.at[d, s - 1, k], r_zb.at[d, s - 1, k], at(x, q, y, zof(1 - d, 1)))
+        return send(src, where, s_ring, r_zb.at[d, s - 1, k], at(x, q, y, zof(1 - d, 1)))
 
     def zb_got(d, s, k):
-        got(e.at[zof(d, s), slot(0, k), zb_rows(d, s)], s_zb.at[d, s - 1, k], r_zb.at[d, s - 1, k])
+        got(e.at[zof(d, s), slot(0, k), zb_rows(d, s)], r_zb.at[d, s - 1, k])
 
     def ya(k):
         where = e.at[z, slot(0, k), pl.ds(0, HEAD)]
         src = emb.at[pl.ds(0, HEAD)] if k == 0 else where
-        return send(src, where, s_ya.at[k], r_ya.at[k], at(x, q, other_y, z))
+        return send(src, where, s_ring, r_ya.at[k], at(x, q, other_y, z))
 
     def ya_got(k):
-        got(e.at[z, slot(1, k), pl.ds(0, HEAD)], s_ya.at[k], r_ya.at[k])
+        got(e.at[z, slot(1, k), pl.ds(0, HEAD)], r_ya.at[k])
 
     def yb(d, s, k):
         where = e.at[zof(d, s), slot(0, k), zb_rows(d, s)]
         src = emb.at[zb_rows(d, s)] if (s, k) == (0, 0) else where
-        return send(src, where, s_yb.at[d, s, k], r_yb.at[d, s, k], at(x, q, other_y, z))
+        return send(src, where, s_ring, r_yb.at[d, s, k], at(x, q, other_y, z))
 
     def yb_got(d, s, k):
-        got(e.at[zof(d, s), slot(1, k), zb_rows(d, s)], s_yb.at[d, s, k], r_yb.at[d, s, k])
+        got(e.at[zof(d, s), slot(1, k), zb_rows(d, s)], r_yb.at[d, s, k])
 
     def la(d, s):
         where = e.at[zof(d, s), :, pl.ds(0, HEAD)]
-        return send(where, where, s_la.at[d, s], r_la.at[d, s], at(x, 1 - q, y, z))
+        return send(where, where, s_l, r_la.at[d, s], at(x, 1 - q, y, z))
 
     def lb(d, s):
         where = e.at[zof(d, s), :, pl.ds(HEAD, ROWS - HEAD)]
-        return send(where, where, s_lb.at[d, s], r_lb.at[d, s], at(x, 1 - q, y, z))
+        return send(where, where, s_l, r_lb.at[d, s], at(x, 1 - q, y, z))
+
+    def l4z():
+        where = e.at[zof(0, 4), pl.ds(2 * pair, 2), pl.ds(HEAD, ROWS - HEAD)]
+        return send(where, where, s_l, r_lb.at[0, 4], at(x, 1 - q, y, z))
+
+    def l4y(d, k):
+        where = e.at[zof(d, 4), slot(1, k), zb_rows(d, 4)]
+        return send(where, where, s_l, r_l4.at[d, k], at(x, 1 - q, y, z))
 
     def dirs(s):
         return (0,) if s in (0, 4) else (0, 1)
@@ -119,7 +130,7 @@
         far = (n + 1) // 2
         return (z + NZ + far * (1 - 2 * (n % 2))) % NZ
 
-    def sel_send(n, k, act, y_to):
+    def sel_send(n, k, y_to):
         zo = zon(n)
         to = at(SLOT_Y[k], zo // 4, y_to, z)
         same = (to[0] == dp) & (to[1] == ce)
@@ -127,29 +138,23 @@
 
         @pl.when(jnp.logical_not(same))
         def _():
-            cp = send(src, dst, s_sel.at[n, k], r_sel.at[group, zo % 4], to)
-            cp.start() if act == "start" else cp.wait_send()
-
-        if act == "start":
-
-            @pl.when(same)
-            def _():
-                pltpu.make_async_copy(src, dst, r_sel.at[group, zo % 4]).start()
-
-    def ids_send(n, act, y_to):
+            send(src, dst, s_sel, r_sel, to).start()
+
+        @pl.when(same)
+        def _():
+            pltpu.make_async_copy(src, dst, r_sel).start()
+
+    def ids_send(n, y_to):
         to = at(n // 2, n % 2, y_to, z)
         same = (to[0] == dp) & (to[1] == ce)
 
         @pl.when(jnp.logical_not(same))
         def _():
-            cp = send(ids_out, ids_in.at[group], s_ids.at[n], r_ids.at[group], to)
-            cp.start() if act == "start" else cp.wait_send()
-
-        if act == "start":
-
-            @pl.when(same)
-            def _():
-                pltpu.make_async_copy(ids_out, ids_in.at[group], r_ids.at[group]).start()
+            send(ids_out, ids_in.at[group], s_ids, r_ids, to).start()
+
+        @pl.when(same)
+        def _():
+            pltpu.make_async_copy(ids_out, ids_in.at[group], r_ids).start()
 
     def choose(a_ref, y_to):
         a = a_ref[...] - CENT * (NZ * y_to + z)
@@ -194,7 +199,7 @@
             zo = zon(n)
             for k in range(4):
                 sel[zo, k] = dot(pick[...], e[zo, k], NN).astype(BF16)
-                sel_send(n, k, "start", y_to)
+                sel_send(n, k, y_to)
 
     def score(lo, hi):
         def one(n):
@@ -254,14 +259,14 @@
         all_c.start()
         own_asg.wait()
         give_asg.start()
-        got(e.at[z, slot(0, 1), pl.ds(0, HEAD)], s_ext.at[0], r_ext.at[0])
+        got(e.at[z, slot(0, 1), pl.ds(0, HEAD)], r_ext.at[0])
         ya(1).start()
         for d in (0, 1):
             za(d, 1, 0, 1).start()
         ya_got(0)
         for d in (0, 1):
             za(d, 1, 1, 0).start()
-        got(e.at[z, slot(0, 1), pl.ds(HEAD, ROWS - HEAD)], s_ext.at[1], r_ext.at[1])
+        got(e.at[z, slot(0, 1), pl.ds(HEAD, ROWS - HEAD)], r_ext.at[1])
         for d in (0, 1):
             zb(d, 1, 1).start()
         yb(0, 0, 1).start()
@@ -270,6 +275,14 @@
             za(d, 1, 1, 1).start()
         own.wait()
         la(0, 0).start()
+        def finish(s):
+            for d in dirs(s):
+                for k in (0, 1):
+                    yb_got(d, s, k)
+                lb(d, s).start()
+            choose_rows(*blocks(s), y)
+            score(*blocks(s))
+
         for s in range(1, 5):
             for k in (0, 1):
                 for d in (0, 1):
@@ -280,7 +293,10 @@
             if s == 1:
                 choose(asg, y)
                 for n in range(8):
-                    ids_send(n, "start", y)
+                    ids_send(n, y)
+            if s == 4:
+                l4z().start()
+                finish(3)
             for b, k in ((0, 0), (0, 1), (1, 0), (1, 1)):
                 for d in (0, 1):
                     za_got(d, s, b, k)
@@ -288,26 +304,31 @@
                         za(d, s + 1, b, k).start()
             for d in dirs(s):
                 la(d, s).start()
-            for d in dirs(s - 1):
-                for k in (0, 1):
-                    yb_got(d, s - 1, k)
-                lb(d, s - 1).start()
             if s == 1:
                 all_c.wait()
                 norms(0, NX)
-            choose_rows(*blocks(s - 1), y)
-            score(*blocks(s - 1))
-        for d in (0, 1):
-            for k in (0, 1):
+            if s < 4:
+                finish(s - 1)
+        for k in (0, 1):
+            for d in (0, 1):
                 yb_got(d, 4, k)
-        lb(0, 4).start()
-        choose_rows(*blocks(4), y)
+                l4y(d, k).start()
         score(*blocks(4))
         top_rows()
-        got(best_leaf, s_bl, r_bl)
+        got(best_leaf, r_bl)
         best_z[z] = jnp.maximum(best[...], best_leaf[...])
         for k in range(1, NZ):
-            send(best_z.at[z], best_z.at[z], s_bz.at[k], r_bz.at[k], at(x, q, y, (z + k) % NZ)).start()
+            send(best_z.at[z], best_z.at[z], s_bz, r_bz, at(x, q, y, (z + k) % NZ)).start()
+        choose_rows(*blocks(4), y)
+        sent(e.at[:, :, pl.ds(0, 960)], s_ring)
+        sent(e, s_l)
+        sent(asg, s_asg)
+        got(best_z.at[pl.ds(0, NZ - 1)], r_bz)
+        m = best_z[0]
+        for k in range(1, NZ):
+            m = jnp.maximum(m, best_z[k])
+        best_y[y % 2] = m
+        tell("start")
 
     @pl.when(jnp.logical_not(is_hub))
     def _():
@@ -319,17 +340,17 @@
             return pl.ds(pl.multiple_of(((x + n) % NX) * QUART + k * PIECE, PIECE), PIECE)
 
         def cross(k):
-            return send(cen.at[part(0, k)], c.at[part(0, k)], s_cc.at[k], r_cc.at[k], at(x, 1 - q, across, z))
+            return send(cen.at[part(0, k)], c.at[part(0, k)], s_c, r_cc.at[k], at(x, 1 - q, across, z))
 
         def near(d, k):
             to = at((x + 1 + 2 * d) % NX, q, y, z)
-            return send(c.at[part(0, k)], c.at[part(0, k)], s_x1.at[d, k], r_x1.at[d, k], to)
+            return send(c.at[part(0, k)], c.at[part(0, k)], s_c, r_x1.at[d, k], to)
 
         def far(k):
             d = k // (PIECES // 2)
             to = at((x + 1 + 2 * d) % NX, q, y, z)
             which = part(3 - 2 * d, k)
-            return send(c.at[which], c.at[which], s_x2.at[k], r_x2.at[k], to)
+            return send(c.at[which], c.at[which], s_c, r_x2.at[k], to)
 
         ext(0).start()
         ext(1).start()
@@ -338,24 +359,31 @@
             ext(n).wait_send()
         for k in range(PIECES):
             cross(k).start()
-        got(asg_in, s_asg, r_asg)
+        got(asg_in, r_asg)
         choose(asg_in, across)
         for n in range(8):
-            ids_send(n, "start", across)
+            ids_send(n, across)
 
         def pass_on(k):
             for d in (0, 1):
-                got(c.at[part(3 - 2 * d, k)], s_x1.at[d, k], r_x1.at[d, k])
+                got(c.at[part(3 - 2 * d, k)], r_x1.at[d, k])
             far(k).start()
 
         def arrived(s):
             for d in dirs(s):
-                got(e.at[zof(d, s), :, pl.ds(0, HEAD)], s_la.at[d, s], r_la.at[d, s])
-                got(e.at[zof(d, s), :, pl.ds(HEAD, ROWS - HEAD)], s_lb.at[d, s], r_lb.at[d, s])
-            choose_rows(*blocks(s), across)
+                got(e.at[zof(d, s), :, pl.ds(0, HEAD)], r_la.at[d, s])
+                if s < 4:
+                    got(e.at[zof(d, s), :, pl.ds(HEAD, ROWS - HEAD)], r_lb.at[d, s])
+                else:
+                    got(e.at[zof(0, 4), pl.ds(2 * pair, 2), pl.ds(HEAD, ROWS - HEAD)], r_lb.at[0, 4])
+                    for k in (0, 1):
+                        for dd in (0, 1):
+                            got(e.at[zof(dd, 4), slot(1, k), zb_rows(dd, 4)], r_l4.at[dd, k])
+            if s < 4:
+                choose_rows(*blocks(s), across)
 
         for k in range(PIECES):
-            got(c.at[part(0, k)], s_cc.at[k], r_cc.at[k])
+            got(c.at[part(0, k)], r_cc.at[k])
             for d in (0, 1):
                 near(d, k).start()
             if k > 1:
@@ -368,7 +396,7 @@
         arrived(1)
         arrived(2)
         for k in range(PIECES):
-            got(c.at[part(2, k)], s_x2.at[k], r_x2.at[k])
+            got(c.at[part(2, k)], r_x2.at[k])
         norms(x + 2, 1)
         score(0, 1)
         score(1, 5)
@@ -378,23 +406,14 @@
         top_rows()
         give = send(best, best_leaf, s_bl, r_bl, at(x, 1 - q, y, z))
         give.start()
-        for k in range(PIECES):
-            cross(k).wait_send()
-            far(k).wait_send()
-            for d in (0, 1):
-                near(d, k).wait_send()
-        for n in range(8):
-            ids_send(n, "wait", across)
-        for n in range(NZ):
-            for k in range(4):
-                sel_send(n, k, "wait", across)
+        choose_rows(*blocks(4), across)
+        sent(c, s_c)
         give.wait_send()
 
     own_slice.wait()
     own_prior.wait()
     pr = prior[...].astype(F32)
-    for n in range(8):
-        got(ids_in.at[n], s_ids.at[n], r_ids.at[n])
+    got(ids_in, r_ids)
     k_of = lax.broadcasted_iota(jnp.int32, (CENT, 128), 0).astype(F32)
     hot = jnp.concatenate(
         [
@@ -405,9 +424,7 @@
     )
     counts = dot(jnp.ones((8, SLICE), BF16), hot, NT)
     den[...] = pr + counts[0:1]
-    for n in range(8):
-        for k in range(4):
-            got(rows.at[n, k], s_sel.at[0, 0], r_sel.at[n, k])
+    got(rows, r_sel)
     for k in range(4):
         f = slice(k * 128, (k + 1) * 128)
         taken = jnp.concatenate([rows[n, k] for n in range(8)], axis=0)
@@ -415,43 +432,18 @@
 
     @pl.when(is_hub)
     def _():
-        for k in range(1, NZ):
-            zs = (z + NZ - k) % NZ
-            got(best_z.at[zs], s_bz.at[k], r_bz.at[k])
-        m = best_z[0]
-        for k in range(1, NZ):
-            m = jnp.maximum(m, best_z[k])
-        best_y[y % 2] = m
-        tell("start")
-        got(best_y.at[1 - y % 2], s_by.at[0], r_by.at[1 - y % 2])
-        for s in range(1, 5):
-            for d in (0, 1):
-                for k in (0, 1):
-                    zb(d, s, k).wait_send()
-                    yb(d, s, k).wait_send()
-                    for b in (0, 1):
-                        za(d, s, b, k).wait_send()
-        for k in (0, 1):
-            ya(k).wait_send()
-            yb(0, 0, k).wait_send()
-        for s in range(5):
-            for d in dirs(s):
-                la(d, s).wait_send()
-                lb(d, s).wait_send()
-        for n in range(NZ):
-            for k in range(4):
-                sel_send(n, k, "wait", y)
-        for n in range(8):
-            ids_send(n, "wait", y)
-        send(asg, asg_in, s_asg, r_asg, at(x, 1 - q, y, z)).wait_send()
-        for k in range(1, NZ):
-            send(best_z.at[z], best_z.at[z], s_bz.at[k], r_bz.at[k], at(x, q, y, (z + k) % NZ)).wait_send()
+        sent(sel.at[pl.ds(0, NZ - 1)], s_sel)
+        sent(ids_in.at[pl.ds(0, 7)], s_ids)
+        sent(best_z.at[pl.ds(0, NZ - 1)], s_bz)
+        got(best_y.at[1 - y % 2], r_by.at[1 - y % 2])
         tell("wait")
 
     @pl.when(jnp.logical_not(is_hub))
     def _():
+        sent(sel, s_sel)
+        sent(ids_in, s_ids)
         for n in (0, 1):
-            got(best_y.at[n], s_by.at[n], r_by.at[n])
+            got(best_y.at[n], r_by.at[n])
 
     top[...] = jnp.maximum(best_y[0], best_y[1])
 
@@ -489,22 +481,14 @@
             pltpu.VMEM((8, 128), F32),
             pltpu.VMEM((NZ, 8, 128), F32),
             pltpu.VMEM((2, 8, 128), F32),
-            *both(2, 4, 2, 2),
-            *both(2, 4, 2),
+            dma(()), dma((2, 4, 2, 2)), dma((2, 4, 2)), dma((2,)), dma((2, 5, 2)),
             *both(2),
-            *both(2, 5, 2),
-            *both(2),
-            *both(2, 5),
-            *both(2, 5),
-            *both(PIECES),
-            *both(2, PIECES),
-            *both(PIECES),
-            dma((NZ, 4)), dma((8, 4)),
-            *both(8),
-            dma(()), dma(()),
-            *both(NZ),
+            dma(()), dma((2, 5)), dma((2, 5)), dma((2, 2)),
+            dma(()), dma((PIECES,)), dma((2, PIECES)), dma((PIECES,)),
+            *both(), *both(),
+            *both(), *both(),
             dma((4,)), dma((2,)),
-            dma(()), dma(()),
+            *both(),
             *both(), *both(), dma(()),
         ],
         compiler_params=pltpu.CompilerParams(

time: 65.9 us -> 63.4 us (0.962)
  Pallas kernels: 63.2 us -> 60.9 us
    pallas_call x1, Pallas kernels: 63.2 us -> 60.9 us  [on_device(): pl.pallas_call(kernel, out_shape=[jax.ShapeDtypeStruct((8, 128), F32), ja...]
where the time goes in v3:
time: 63.4 us; the launch traced here: 63.3 us
  Pallas kernels  60.9 us (96%)
  other arithmetic  1.11 us (2%)
  between operations  0.64 us (1%)
    pallas_call x1, Pallas kernels, on_device(): pl.pallas_call(kernel, out_shape=[jax.ShapeDtypeStruct((8, 128), F32), ja...  60.9 us

profile of v3, /device:TPU:1, one launch (start us, length us, event | category | flops | bytes accessed | tf_op | source)
XLA Modules:
  0.0 63.3 jit_solution(1747629974782059685)
XLA Ops:
  0.6 60.9 %score_and_update.1 = (f32[8,128]{1,0:T(8,128)S(1)}, f32[512,512]{1,0:T(8,128)S(1)}, f32[1,512]{1,0:T(1,128)S(1)}) custom-call(bf16[1024,128]{1,0:T(8,128)(2,1)} %emb.1, bf16[512,4096]{1,0:T(8,128)(2,1)} %cen.1, s32[8,128]{1,0:T(8,128)} %bitcast.6, s32[1,512]{1,0:T(1,128)} %bitcast.7), custom_call_target="tpu_custom_call" | custom-call | tf_op jit(solution)/shard_map/score_and_update/pallas_call | solution.py:457
  61.6 1.1 %broadcast_divide_fusion = f32[512,512]{1,0:T(8,128)} fusion(f32[512,512]{1,0:T(8,128)S(1)} %get-tuple-element.6, f32[512]{0:T(512)S(1)} %bitcast.5), kind=kLoop, calls=%fused_computation | loop fusion | flops 262144 | bytes 2099200 | tf_op jit(solution)/shard_map/div | solution.py:499
  62.7 0.6 copy.7

commit v4 on v3

v4 whole, which is shorter than its diff:
```python
import jax
import jax.numpy as jnp
from jax import lax
from jax.experimental import pallas as pl
from jax.experimental.pallas import tpu as pltpu
from jax.sharding import PartitionSpec as P

NX, NY, NZ = 4, 4, 8
ROWS = 1024
WIDTH = 128
CENT = 512
FEAT = 4096
CAP = 64
SLICE = 512
HEAD = 416
STAGES = 0, 384, 640, 1024
QUART = CENT // NX
PIECES = 8
PIECE = QUART // PIECES
SLOT_Y = (0, 3, 1, 2)
F32, BF16 = jnp.float32, jnp.bfloat16
NT = (((1,), (1,)), ((), ()))
NN = (((1,), (0,)), ((), ()))


def dot(a, b, dims):
    return lax.dot_general(a, b, dims, preferred_element_type=F32)


def kernel(
    emb, cen, asg_hbm, prior_hbm, top, num, den,
    e, c, acc, cs, sel, rows, ids_out, ids_in, asg, prior, pick, hn, best, best_y,
    s_ring, r_za, r_zb, r_ya, r_yb, s_ext, r_ext, s_l, r_la, r_lb, r_l4,
    s_c, r_cc, r_x1, r_x2, s_sel, r_sel, s_ids, r_ids, s_pick, r_pick, s_pick_ids, r_pick_ids, s_by, r_by,
    l_own, l_c, l_cs, l_asg, l_prior,
):
    dp, ce = lax.axis_index("dp"), lax.axis_index("cent")
    x, q, y, z = dp // 2, dp % 2, ce // NZ, ce % NZ
    h = y // 2
    pair = ((y + 1) // 2) % 2
    other_y, across = y + 1 - 2 * (y % 2), 3 - y
    group = 2 * x + h
    is_hub = q == h

    def at(x_, q_, y_, z_):
        return (2 * x_ + q_, NZ * y_ + z_)

    def send(src, dst, ss, rs, dev):
        return pltpu.make_async_remote_copy(
            src_ref=src, dst_ref=dst, send_sem=ss, recv_sem=rs,
            device_id=dev, device_id_type=pl.DeviceIdType.MESH,
        )

    def got(dst, rs):
        send(dst, dst, s_ring, rs, (dp, ce)).wait_recv()

    def sent(src, ss):
        send(src, src, ss, r_pick, (dp, ce)).wait_send()

    def slot(b, k):
        p = pair if b == 0 else 1 - pair
        if k is None:
            return pl.ds(2 * p, 2)
        return 2 * p + (h if k == 0 else 1 - h)

    def zof(d, s):
        return (z + NZ - s) % NZ if d == 0 else (z + s) % NZ

    def zon(n):
        far = (n + 1) // 2
        return (z + NZ + far * (1 - 2 * (n % 2))) % NZ

    def dirs(s):
        return (0,) if s in (0, 4) else (0, 1)

    def za_rows(d, s):
        return pl.ds(0, HEAD) if s < 4 else pl.ds(d * (HEAD // 2), HEAD // 2)

    def zb_rows(d, s):
        n = ROWS - HEAD
        return pl.ds(HEAD, n) if s < 4 else pl.ds(HEAD + d * (n // 2), n // 2)

    def za(d, s, b, k):
        where = e.at[zof(d, s - 1), slot(b, k), za_rows(d, s)]
        src = emb.at[za_rows(d, s)] if (s, b, k) == (1, 0, 0) else where
        return send(src, where, s_ring, r_za.at[d, s - 1, b, k or 0], at(x, q, y, zof(1 - d, 1)))

    def za_got(d, s, b, k):
        got(e.at[zof(d, s), slot(b, k), za_rows(d, s)], r_za.at[d, s - 1, b, k or 0])

    def zb(d, s, k):
        where = e.at[zof(d, s - 1), slot(0, k), zb_rows(d, s)]
        src = emb.at[zb_rows(d, s)] if (s, k) == (1, 0) else where
        return send(src, where, s_ring, r_zb.at[d, s - 1, k or 0], at(x, q, y, zof(1 - d, 1)))

    def zb_got(d, s, k):
        got(e.at[zof(d, s), slot(0, k), zb_rows(d, s)], r_zb.at[d, s - 1, k or 0])

    def ya(k):
        where = e.at[z, slot(0, k), pl.ds(0, HEAD)]
        src = emb.at[pl.ds(0, HEAD)] if k == 0 else where
        return send(src, where, s_ring, r_ya.at[k], at(x, q, other_y, z))

    def ya_got(k):
        got(e.at[z, slot(1, k), pl.ds(0, HEAD)], r_ya.at[k])

    def yb(d, s, k):
        where = e.at[zof(d, s), slot(0, k), zb_rows(d, s)]
        src = emb.at[zb_rows(d, s)] if (s, k) == (0, 0) else where
        return send(src, where, s_ring, r_yb.at[d, s, k or 0], at(x, q, other_y, z))

    def yb_got(d, s, k):
        got(e.at[zof(d, s), slot(1, k), zb_rows(d, s)], r_yb.at[d, s, k or 0])

    def to_leaf(where, rs):
        return send(where, where, s_l, rs, at(x, 1 - q, y, z))

    def la_where(d, s):
        return e.at[zof(d, s), :, pl.ds(0, HEAD)]

    def lb_where(d, s):
        return e.at[zof(d, s), :, pl.ds(HEAD, ROWS - HEAD)]

    def l4z_where():
        return e.at[zof(0, 4), slot(0, None), pl.ds(HEAD, ROWS - HEAD)]

    def l4y_where(d):
        return e.at[zof(d, 4), slot(1, None), zb_rows(d, 4)]

    def send_or_keep(src, dst, ss, rs, to):
        same = (to[0] == dp) & (to[1] == ce)

        @pl.when(jnp.logical_not(same))
        def _():
            send(src, dst, ss, rs, to).start()

        @pl.when(same)
        def _():
            pltpu.make_async_copy(src, dst, rs).start()

    def choose(t, y_to):
        a = asg[...] - CENT * (NZ * y_to + z)
        mask = (a >= 0) & (a < CENT)
        m = jnp.where(mask, 1.0, 0.0).astype(F32)
        mb = m.astype(BF16)
        i0 = lax.broadcasted_iota(jnp.int32, (128, 128), 0)
        i1 = lax.broadcasted_iota(jnp.int32, (128, 128), 1)
        before = dot(mb, jnp.where(i0 < i1, 1.0, 0.0).astype(BF16), NN)
        total = dot(mb, jnp.ones((128, 128), BF16), NN)
        v = jnp.where(mask, a + 1, 0)
        high, low = (v // 32).astype(F32), (v % 32).astype(F32)
        first = lax.broadcasted_iota(jnp.int32, (8, 128), 0) == 0
        rank_of = lax.broadcasted_iota(jnp.int32, (128, 128), 0).astype(F32)
        off = (CAP * h).astype(F32)
        run = jnp.zeros((1, 128), F32)
        ids = jnp.zeros((8, 128), F32)
        for i in range(8):
            here = m[i : i + 1] > 0.5
            rank = before[i : i + 1] + run
            run = run + total[i : i + 1]
            one = jnp.where((rank == rank_of) & here, 1.0, 0.0).astype(BF16)
            pick[CAP * t : CAP * (t + 1), 128 * i : 128 * (i + 1)] = one[:CAP]
            put = jnp.where((rank + off == rank_of) & here, 1.0, 0.0).astype(BF16)
            vals = jnp.where(first, high[i : i + 1], low[i : i + 1]).astype(BF16)
            ids = ids + dot(vals, put, NT)
        ids_out[t] = jnp.broadcast_to(32.0 * ids[0:1] + ids[1:2] - 1.0, (8, 128))

    def norms(first, count, base):
        @pl.loop(0, count)
        def _(i):
            part = jnp.zeros((128, 128), F32)
            r = pl.ds(pl.multiple_of(base + (first + i) % NX * 128, 128), 128)
            for k in range(FEAT // 128):
                v = c[r, k * 128 : (k + 1) * 128].astype(F32)
                part = part + v * v
            hn[r, :] = 0.5 * jnp.sum(part, axis=1, keepdims=True)

    def choose_rows(n):
        zo = zon(n)
        for k in range(4):
            got_rows = dot(pick[...], e[zo, k], NN).astype(BF16)
            for t in (0, 1):
                sel[t, k, zo] = got_rows[CAP * t : CAP * (t + 1)]

    def give_rows(n):
        zo = zon(n)

        def go():
            for k in range(4):
                for t in (0, 1):
                    to = at(SLOT_Y[k], zo // 4, across if t else y, z)
                    src, dst = sel.at[t, k, zo], rows.at[group, zo % 4]
                    if t:
                        send(src, dst, s_sel.at[t], r_sel, to).start()
                    else:
                        send_or_keep(src, dst, s_sel.at[t], r_sel, to)

        if n == NZ - 1:
            go()
        else:
            pl.when(zo // 4 != z // 4)(go)

    def give_half():
        half = z // 4
        for k in range(4):
            for t in (0, 1):
                to = at(SLOT_Y[k], half, across if t else y, z)
                src, dst = sel.at[t, k, pl.ds(4 * half, 4)], rows.at[group]
                if t:
                    send(src, dst, s_sel.at[t], r_sel, to).start()
                else:
                    send_or_keep(src, dst, s_sel.at[t], r_sel, to)

    def product(n, r, cr):
        zo = zon(n)
        left = jnp.concatenate(
            [c[cr, pl.ds(pl.multiple_of(yy * 1024 + zo * 128, 128), 128)] for yy in SLOT_Y], axis=1
        )
        return dot(left, jnp.concatenate([e[zo, k, r] for k in range(4)], axis=1), NT)

    def score(n, t):
        cr = slice(CENT * t, CENT * (t + 1))
        if n == 0:
            acc[cr] = product(0, slice(None), cr)
        else:
            acc[cr] += product(n, slice(None), cr)

    def last_score(stage):
        lo, hi = STAGES[stage : stage + 2]
        r = slice(lo, hi)
        m = jnp.max(acc[:, r] + product(NZ - 1, r, slice(None)) - hn[...], axis=0, keepdims=True)
        for i in range(lo // 128, hi // 128):
            best[i : i + 1, :] = m[:, 128 * i - lo : 128 * (i + 1) - lo]

    barrier = pltpu.get_barrier_semaphore()
    own_slice = pltpu.make_async_copy(cen.at[:, pl.ds(pl.multiple_of(dp * SLICE, SLICE), SLICE)], cs, l_cs)
    own_asg = pltpu.make_async_copy(asg_hbm, asg, l_asg)
    own_prior = pltpu.make_async_copy(prior_hbm, prior, l_prior)
    own = pltpu.make_async_copy(emb, e.at[z, slot(0, 0)], l_own)
    own_c = pltpu.make_async_copy(cen, c.at[pl.ds(0, CENT)], l_c)
    own_prior.start()
    own_slice.start()
    peers = [(dp, NZ * y + (z + 1) % NZ), (dp, NZ * y + (z + NZ - 1) % NZ), (dp, NZ * other_y + z)]
    peers += [at(x, 1 - q, y, z), at(x, 1 - q, across, z), (dp, NZ * across + z)]
    peers += [((dp + 2) % 8, ce), ((dp + 6) % 8, ce)]
    for to in peers:
        pl.semaphore_signal(barrier, inc=1, device_id=to, device_id_type=pl.DeviceIdType.MESH)

    @pl.when(is_hub)
    def _():
        own_asg.start()
        own.start()

    @pl.when(jnp.logical_not(is_hub))
    def _():
        own_c.start()

    pl.semaphore_wait(barrier, len(peers))

    @pl.when(is_hub)
    def _():
        for d in (0, 1):
            zb(d, 1, 0).start()
        for d in (0, 1):
            za(d, 1, 0, 0).start()
        ya(0).start()
        yb(0, 0, 0).start()
        got(e.at[z, slot(0, 1), pl.ds(0, HEAD)], r_ext.at[0])
        ya(1).start()
        for d in (0, 1):
            za(d, 1, 0, 1).start()
        ya_got(0)
        for d in (0, 1):
            za(d, 1, 1, 0).start()
        own_asg.wait()
        choose(0, y)
        got(e.at[z, slot(0, 1), pl.ds(HEAD, ROWS - HEAD)], r_ext.at[1])
        for d in (0, 1):
            zb(d, 1, 1).start()
        yb(0, 0, 1).start()
        ya_got(1)
        for d in (0, 1):
            za(d, 1, 1, 1).start()
        own.wait()
        to_leaf(la_where(0, 0), r_la.at[0, 0]).start()
        choose(1, across)
        send(pick, pick, s_pick, r_pick, at(x, 1 - q, y, z)).start()
        send(ids_out, ids_out, s_pick_ids, r_pick_ids, at(x, 1 - q, y, z)).start()

        def y_done(s):
            for d in dirs(s):
                for k in (0, 1) if s < 2 else (None,):
                    yb_got(d, s, k)
                to_leaf(lb_where(d, s), r_lb.at[d, s]).start()

        for k in (0, 1, None):
            for d in (0, 1):
                if k is not None:
                    zb_got(d, 1, k)
                    yb(d, 1, k).start()
                    if k == 1:
                        zb(d, 2, None).start()
            if k == 0:
                for d in (0, 1):
                    for kk in (0, 1):
                        za_got(d, 1, 0, kk)
                    za(d, 2, 0, None).start()
                for d in (0, 1):
                    za_got(d, 1, 1, 0)
            elif k is None:
                for d in (0, 1):
                    za_got(d, 1, 1, 1)
                    za(d, 2, 1, None).start()
        for d in (0, 1):
            to_leaf(la_where(d, 1), r_la.at[d, 1]).start()
        y_done(0)
        for s in range(2, 5):
            for d in (0, 1):
                zb_got(d, s, None)
                if s < 4:
                    zb(d, s + 1, None).start()
                yb(d, s, None).start()
            if s == 4:
                to_leaf(l4z_where(), r_lb.at[0, 4]).start()
            for d in (0, 1):
                za_got(d, s, 0, None)
                if s < 4:
                    za(d, s + 1, 0, None).start()
            y_done(s - 1)
            for d in (0, 1):
                za_got(d, s, 1, None)
                if s < 4:
                    za(d, s + 1, 1, None).start()
            for d in dirs(s):
                to_leaf(la_where(d, s), r_la.at[d, s]).start()
        for d in (0, 1):
            yb_got(d, 4, None)
            to_leaf(l4y_where(d), r_l4.at[d]).start()
        sent(e.at[:, :, pl.ds(0, 960)], s_ring)
        sent(e, s_l)
        sent(pick, s_pick)
        sent(ids_out, s_pick_ids)

    @pl.when(jnp.logical_not(is_hub))
    def _():
        def ext(n):
            r = pl.ds(0, HEAD) if n == 0 else pl.ds(HEAD, ROWS - HEAD)
            return send(emb.at[r], e.at[z, slot(0, 0), r], s_ext.at[n], r_ext.at[n], at(x, q, across, z))

        def part(n, k, base=CENT):
            return pl.ds(pl.multiple_of(base + ((x + n) % NX) * QUART + k * PIECE, PIECE), PIECE)

        def cross(k):
            return send(cen.at[part(0, k, 0)], c.at[part(0, k)], s_c, r_cc.at[k], at(x, 1 - q, across, z))

        def near(d, k):
            to = at((x + 1 + 2 * d) % NX, q, y, z)
            return send(c.at[part(0, k)], c.at[part(0, k)], s_c, r_x1.at[d, k], to)

        def far(k):
            d = k // (PIECES // 2)
            to = at((x + 1 + 2 * d) % NX, q, y, z)
            which = part(3 - 2 * d, k)
            return send(c.at[which], c.at[which], s_c, r_x2.at[k], to)

        def pass_on(k):
            for d in (0, 1):
                got(c.at[part(3 - 2 * d, k)], r_x1.at[d, k])
            far(k).start()

        def arrived(s, n):
            d = n % 2 if s == 0 else (n + 1) % 2
            got(la_where(d, s), r_la.at[d, s])
            got(lb_where(d, s), r_lb.at[d, s])
            choose_rows(n)
            score(n, 0)

        ext(0).start()
        ext(1).start()
        for n in (0, 1):
            ext(n).wait_send()
        for k in range(PIECES):
            cross(k).start()
        own_c.wait()
        norms(0, NX, 0)
        for k in range(PIECES):
            got(c.at[part(0, k)], r_cc.at[k])
            for d in (0, 1):
                near(d, k).start()
            if k > 1:
                pass_on(k - 2)
            if k == 3:
                got(pick, r_pick)
                arrived(0, 0)
        arrived(1, 1)
        for k in range(PIECES - 2, PIECES):
            pass_on(k)
        arrived(1, 2)
        norms(x, 2, CENT)
        norms(x + 3, 1, CENT)
        arrived(2, 3)
        arrived(2, 4)
        for k in range(PIECES):
            got(c.at[part(2, k)], r_x2.at[k])
        got(ids_out, r_pick_ids)
        for n in range(8):
            send_or_keep(ids_out.at[0], ids_in.at[group], s_ids.at[0], r_ids, at(n // 2, n % 2, y, z))
            send(ids_out.at[1], ids_in.at[group], s_ids.at[1], r_ids, at(n // 2, n % 2, across, z)).start()
        for n in range(1, 5):
            give_rows(n)
        norms(x + 2, 1, CENT)
        for n in range(5):
            score(n, 1)
        for n in (5, 6):
            arrived(3, n)
            give_rows(n)
            score(n, 1)
        give_half()
        got(la_where(0, 4), r_la.at[0, 4])
        last_score(0)
        got(l4z_where(), r_lb.at[0, 4])
        for d in (0, 1):
            got(l4y_where(d), r_l4.at[d])
            last_score(d + 1)
        for k in (4, 3, 5, 2, 6, 1, 7, 0):
            for yy in (3 - other_y, across, other_y, y):
                to = at(x, h, yy, (z + k) % NZ)
                send(best, best_y.at[y % 2, z], s_by, r_by, to).start()
        choose_rows(NZ - 1)
        give_rows(NZ - 1)
        sent(c.at[pl.ds(0, CENT)], s_c)

    own_slice.wait()
    own_prior.wait()
    pr = prior[...].astype(F32)
    got(ids_in, r_ids)
    k_of = lax.broadcasted_iota(jnp.int32, (CENT, 128), 0).astype(F32)
    hot = jnp.concatenate(
        [
            jnp.where(jnp.maximum(ids_in[2 * n, 0:1], ids_in[2 * n + 1, 0:1]) == k_of, 1.0, 0.0).astype(BF16)
            for n in range(4)
        ],
        axis=1,
    )
    counts = dot(jnp.ones((8, SLICE), BF16), hot, NT)
    den[...] = pr + counts[0:1]
    for k in range(4):
        f = slice(k * 128, (k + 1) * 128)
        num[f, :] = pr * cs[:, f].astype(F32).T
    got(rows, r_sel)
    for k in range(4):
        f = slice(k * 128, (k + 1) * 128)
        taken = jnp.concatenate([rows[n, k] for n in range(8)], axis=0)
        num[f, :] += dot(taken.T, hot, NT)

    @pl.when(jnp.logical_not(is_hub))
    def _():
        sent(sel.at[0, :, pl.ds(0, NZ - 1)], s_sel.at[0])
        sent(sel.at[1], s_sel.at[1])
        sent(ids_in.at[pl.ds(0, 7)], s_ids.at[0])
        sent(ids_in, s_ids.at[1])
        sent(e.at[0, 0, pl.ds(0, 512)], s_by)

    got(best_y, r_by)
    m = best_y[0, 0]
    for n in range(1, 2 * NZ):
        m = jnp.maximum(m, best_y[n // NZ, n % NZ])
    top[...] = m


def on_device(embeddings, centroids, assignment, prior_counts):
    dma = pltpu.SemaphoreType.DMA
    both = lambda *shape: [dma(shape), dma(shape)]
    vmem, hbm = pl.BlockSpec(memory_space=pltpu.VMEM), pl.BlockSpec(memory_space=pltpu.HBM)
    placed = (embeddings, centroids, assignment.reshape(8, 128), prior_counts.reshape(1, CENT))
    placed = [pltpu.with_memory_space_constraint(v, pltpu.HBM) for v in placed]
    top, num, den = pl.pallas_call(
        kernel,
        out_shape=[
            jax.ShapeDtypeStruct((8, 128), F32),
            jax.ShapeDtypeStruct((SLICE, CENT), F32),
            jax.ShapeDtypeStruct((1, CENT), F32),
        ],
        in_specs=[hbm, hbm, hbm, hbm],
        out_specs=[vmem, vmem, vmem],
        scratch_shapes=[
            pltpu.VMEM((NZ, 4, ROWS, WIDTH), BF16),
            pltpu.VMEM((2 * CENT, FEAT), BF16),
            pltpu.VMEM((2 * CENT, ROWS), F32),
            pltpu.VMEM((CENT, SLICE), BF16),
            pltpu.VMEM((2, 4, NZ, CAP, WIDTH), BF16),
            pltpu.VMEM((8, 4, CAP, WIDTH), BF16),
            pltpu.VMEM((2, 8, 128), F32),
            pltpu.VMEM((8, 8, 128), F32),
            pltpu.VMEM((8, 128), jnp.int32),
            pltpu.VMEM((1, CENT), jnp.int32),
            pltpu.VMEM((2 * CAP, ROWS), BF16),
            pltpu.VMEM((2 * CENT, 1), F32),
            pltpu.VMEM((8, 128), F32),
            pltpu.VMEM((2, NZ, 8, 128), F32),
            dma(()), dma((2, 4, 2, 2)), dma((2, 4, 2)), dma((2,)), dma((2, 5, 2)),
            *both(2),
            dma(()), dma((2, 5)), dma((2, 5)), dma((2,)),
            dma(()), dma((PIECES,)), dma((2, PIECES)), dma((PIECES,)),
            dma((2,)), dma(()),
            dma((2,)), dma(()),
            *both(), *both(), *both(),
            *both(), *both(), dma(()),
        ],
        compiler_params=pltpu.CompilerParams(
            collective_id=0, has_side_effects=True, vmem_limit_bytes=40 * 2**20
        ),
        name="score_and_update",
    )(*placed)
    return top.reshape(ROWS), num / den


def solution(mesh):
    placed = (P("dp", "cent"), P("cent", None), P("dp"), P("cent"))
    return jax.shard_map(
        on_device, mesh=mesh, in_specs=placed, out_specs=(P("dp"), P("dp", "cent")), check_vma=False
    )
```

time: 63.4 us -> 60.3 us (0.951)
  Pallas kernels: 60.9 us -> 57.8 us
    pallas_call x1, Pallas kernels: 60.9 us -> 57.8 us  [on_device(): pl.pallas_call(kernel, out_shape=[jax.ShapeDtypeStruct((8, 128), F32), ja...]
where the time goes in v4:
time: 60.3 us; the launch traced here: 60.2 us
  Pallas kernels  57.8 us (96%)
  other arithmetic  1.11 us (2%)
  between operations  0.64 us (1%)
    pallas_call x1, Pallas kernels, on_device(): pl.pallas_call(kernel, out_shape=[jax.ShapeDtypeStruct((8, 128), F32), ja...  57.8 us

profile of v4, /device:TPU:1, one launch (start us, length us, event | category | flops | bytes accessed | tf_op | source)
XLA Modules:
  0.0 60.2 jit_solution(3234506590855861989)
XLA Ops:
  0.6 57.8 %score_and_update.1 = (f32[8,128]{1,0:T(8,128)S(1)}, f32[512,512]{1,0:T(8,128)S(1)}, f32[1,512]{1,0:T(1,128)S(1)}) custom-call(bf16[1024,128]{1,0:T(8,128)(2,1)} %emb.1, bf16[512,4096]{1,0:T(8,128)(2,1)} %cen.1, s32[8,128]{1,0:T(8,128)} %bitcast.6, s32[1,512]{1,0:T(1,128)} %bitcast.7), custom_call_target="tpu_custom_call" | custom-call | tf_op jit(solution)/shard_map/score_and_update/pallas_call | solution.py:477
  58.5 1.1 %broadcast_divide_fusion = f32[512,512]{1,0:T(8,128)} fusion(f32[512,512]{1,0:T(8,128)S(1)} %get-tuple-element.6, f32[512]{0:T(512)S(1)} %bitcast.5), kind=kLoop, calls=%fused_computation | loop fusion | flops 262144 | bytes 2099200 | tf_op jit(solution)/shard_map/div | solution.py:515
  59.6 0.6 copy.7

commit v5 on v4

--- a/solution.py
+++ b/solution.py
@@ -12,7 +12,7 @@
 FEAT = 4096
 CAP = 64
 SLICE = 512
-HEAD = 416
+HEAD = 480
 STAGES = 0, 384, 640, 1024
 QUART = CENT // NX
 PIECES = 8
@@ -29,10 +29,10 @@
 
 def kernel(
     emb, cen, asg_hbm, prior_hbm, top, num, den,
-    e, c, acc, cs, sel, rows, ids_out, ids_in, asg, prior, pick, hn, best, best_y,
+    e, c, acc, cs, sel, spare, rows, ids_out, ids_in, asg, prior, pick, hn, best, best_y,
     s_ring, r_za, r_zb, r_ya, r_yb, s_ext, r_ext, s_l, r_la, r_lb, r_l4,
-    s_c, r_cc, r_x1, r_x2, s_sel, r_sel, s_ids, r_ids, s_pick, r_pick, s_pick_ids, r_pick_ids, s_by, r_by,
-    l_own, l_c, l_cs, l_asg, l_prior,
+    s_c, r_cc, r_x1, r_x2, s_sel, r_sel, s_ids, r_ids, s_by, r_by,
+    l_own, l_c, l_cs, l_asg, l_prior, ready,
 ):
     dp, ce = lax.axis_index("dp"), lax.axis_index("cent")
     x, q, y, z = dp // 2, dp % 2, ce // NZ, ce % NZ
@@ -55,7 +55,7 @@
         send(dst, dst, s_ring, rs, (dp, ce)).wait_recv()
 
     def sent(src, ss):
-        send(src, src, ss, r_pick, (dp, ce)).wait_send()
+        send(src, src, ss, r_by, (dp, ce)).wait_send()
 
     def slot(b, k):
         p = pair if b == 0 else 1 - pair
@@ -127,7 +127,7 @@
     def l4y_where(d):
         return e.at[zof(d, 4), slot(1, None), zb_rows(d, 4)]
 
-    def send_or_keep(src, dst, ss, rs, to):
+    def send_or_keep(src, dst, ss, rs, to, spare=None):
         same = (to[0] == dp) & (to[1] == ce)
 
         @pl.when(jnp.logical_not(same))
@@ -137,6 +137,8 @@
         @pl.when(same)
         def _():
             pltpu.make_async_copy(src, dst, rs).start()
+            if spare is not None:
+                pltpu.make_async_copy(src, spare, ss).start()
 
     def choose(t, y_to):
         a = asg[...] - CENT * (NZ * y_to + z)
@@ -184,32 +186,14 @@
 
     def give_rows(n):
         zo = zon(n)
-
-        def go():
-            for k in range(4):
-                for t in (0, 1):
-                    to = at(SLOT_Y[k], zo // 4, across if t else y, z)
-                    src, dst = sel.at[t, k, zo], rows.at[group, zo % 4]
-                    if t:
-                        send(src, dst, s_sel.at[t], r_sel, to).start()
-                    else:
-                        send_or_keep(src, dst, s_sel.at[t], r_sel, to)
-
-        if n == NZ - 1:
-            go()
-        else:
-            pl.when(zo // 4 != z // 4)(go)
-
-    def give_half():
-        half = z // 4
         for k in range(4):
             for t in (0, 1):
-                to = at(SLOT_Y[k], half, across if t else y, z)
-                src, dst = sel.at[t, k, pl.ds(4 * half, 4)], rows.at[group]
+                to = at(SLOT_Y[k], zo // 4, across if t else y, z)
+                src, dst = sel.at[t, k, zo], rows.at[group, zo % 4]
                 if t:
                     send(src, dst, s_sel.at[t], r_sel, to).start()
                 else:
-                    send_or_keep(src, dst, s_sel.at[t], r_sel, to)
+                    send_or_keep(src, dst, s_sel.at[t], r_sel, to, spare.at[n])
 
     def product(n, r, cr):
         zo = zon(n)
@@ -284,8 +268,6 @@
         own.wait()
         to_leaf(la_where(0, 0), r_la.at[0, 0]).start()
         choose(1, across)
-        send(pick, pick, s_pick, r_pick, at(x, 1 - q, y, z)).start()
-        send(ids_out, ids_out, s_pick_ids, r_pick_ids, at(x, 1 - q, y, z)).start()
 
         def y_done(s):
             for d in dirs(s):
@@ -316,17 +298,34 @@
         y_done(0)
         for s in range(2, 5):
             for d in (0, 1):
-                zb_got(d, s, None)
-                if s < 4:
-                    zb(d, s + 1, None).start()
-                yb(d, s, None).start()
+                for k in (None,) if s < 4 else (0, 1):
+                    zb_got(d, s, k)
+                    if s < 3:
+                        zb(d, s + 1, k).start()
+                    elif s == 3:
+                        zb(d, 4, 0).start()
+                        zb(d, 4, 1).start()
+                    yb(d, s, k).start()
             if s == 4:
                 to_leaf(l4z_where(), r_lb.at[0, 4]).start()
+                y_done(3)
+                pl.semaphore_wait(ready, 1)
+                for n in range(8):
+                    send_or_keep(ids_out.at[0], ids_in.at[group], s_ids.at[0], r_ids, at(n // 2, n % 2, y, z))
+                    send(ids_out.at[1], ids_in.at[group], s_ids.at[1], r_ids, at(n // 2, n % 2, across, z)).start()
+                for n in range(7):
+                    if n > 4:
+                        choose_rows(n)
+                    give_rows(n)
             for d in (0, 1):
                 za_got(d, s, 0, None)
                 if s < 4:
                     za(d, s + 1, 0, None).start()
-            y_done(s - 1)
+            if s < 4:
+                y_done(s - 1)
+            if s == 3:
+                for n in range(5):
+                    choose_rows(n)
             for d in (0, 1):
                 za_got(d, s, 1, None)
                 if s < 4:
@@ -334,12 +333,13 @@
             for d in dirs(s):
                 to_leaf(la_where(d, s), r_la.at[d, s]).start()
         for d in (0, 1):
-            yb_got(d, 4, None)
+            yb_got(d, 4, 0)
+            yb_got(d, 4, 1)
             to_leaf(l4y_where(d), r_l4.at[d]).start()
+        choose_rows(7)
+        give_rows(7)
         sent(e.at[:, :, pl.ds(0, 960)], s_ring)
         sent(e, s_l)
-        sent(pick, s_pick)
-        sent(ids_out, s_pick_ids)
 
     @pl.when(jnp.logical_not(is_hub))
     def _():
@@ -372,7 +372,6 @@
             d = n % 2 if s == 0 else (n + 1) % 2
             got(la_where(d, s), r_la.at[d, s])
             got(lb_where(d, s), r_lb.at[d, s])
-            choose_rows(n)
             score(n, 0)
 
         ext(0).start()
@@ -390,7 +389,6 @@
             if k > 1:
                 pass_on(k - 2)
             if k == 3:
-                got(pick, r_pick)
                 arrived(0, 0)
         arrived(1, 1)
         for k in range(PIECES - 2, PIECES):
@@ -402,20 +400,13 @@
         arrived(2, 4)
         for k in range(PIECES):
             got(c.at[part(2, k)], r_x2.at[k])
-        got(ids_out, r_pick_ids)
-        for n in range(8):
-            send_or_keep(ids_out.at[0], ids_in.at[group], s_ids.at[0], r_ids, at(n // 2, n % 2, y, z))
-            send(ids_out.at[1], ids_in.at[group], s_ids.at[1], r_ids, at(n // 2, n % 2, across, z)).start()
-        for n in range(1, 5):
-            give_rows(n)
+        pl.semaphore_signal(ready, inc=1, device_id=at(x, h, y, z), device_id_type=pl.DeviceIdType.MESH)
         norms(x + 2, 1, CENT)
         for n in range(5):
             score(n, 1)
         for n in (5, 6):
             arrived(3, n)
-            give_rows(n)
             score(n, 1)
-        give_half()
         got(la_where(0, 4), r_la.at[0, 4])
         last_score(0)
         got(l4z_where(), r_lb.at[0, 4])
@@ -426,8 +417,6 @@
             for yy in (3 - other_y, across, other_y, y):
                 to = at(x, h, yy, (z + k) % NZ)
                 send(best, best_y.at[y % 2, z], s_by, r_by, to).start()
-        choose_rows(NZ - 1)
-        give_rows(NZ - 1)
         sent(c.at[pl.ds(0, CENT)], s_c)
 
     own_slice.wait()
@@ -455,11 +444,14 @@
 
     @pl.when(jnp.logical_not(is_hub))
     def _():
-        sent(sel.at[0, :, pl.ds(0, NZ - 1)], s_sel.at[0])
-        sent(sel.at[1], s_sel.at[1])
+        sent(e.at[0, 0, pl.ds(0, 512)], s_by)
+
+    @pl.when(is_hub)
+    def _():
         sent(ids_in.at[pl.ds(0, 7)], s_ids.at[0])
         sent(ids_in, s_ids.at[1])
-        sent(e.at[0, 0, pl.ds(0, 512)], s_by)
+        for t in (0, 1):
+            sent(sel.at[t], s_sel.at[t])
 
     got(best_y, r_by)
     m = best_y[0, 0]
@@ -489,6 +481,7 @@
             pltpu.VMEM((2 * CENT, ROWS), F32),
             pltpu.VMEM((CENT, SLICE), BF16),
             pltpu.VMEM((2, 4, NZ, CAP, WIDTH), BF16),
+            pltpu.VMEM((NZ, CAP, WIDTH), BF16),
             pltpu.VMEM((8, 4, CAP, WIDTH), BF16),
             pltpu.VMEM((2, 8, 128), F32),
             pltpu.VMEM((8, 8, 128), F32),
@@ -504,8 +497,8 @@
             dma(()), dma((PIECES,)), dma((2, PIECES)), dma((PIECES,)),
             dma((2,)), dma(()),
             dma((2,)), dma(()),
-            *both(), *both(), *both(),
-            *both(), *both(), dma(()),
+            *both(),
+            *both(), *both(), dma(()), pltpu.SemaphoreType.REGULAR,
         ],
         compiler_params=pltpu.CompilerParams(
             collective_id=0, has_side_effects=True, vmem_limit_bytes=40 * 2**20

time: 60.3 us -> 58.5 us (0.970)
  Pallas kernels: 57.8 us -> 56.1 us
    pallas_call x1, Pallas kernels: 57.8 us -> 56.1 us  [on_device(): pl.pallas_call(kernel, out_shape=[jax.ShapeDtypeStruct((8, 128), F32), ja...]
where the time goes in v5:
time: 58.5 us
  Pallas kernels  56.1 us (96%)
  other arithmetic  1.11 us (2%)
  between operations  0.64 us (1%)
  local copies, waits for them, and re-layouts  0.59 us (1%)
    pallas_call x1, Pallas kernels, on_device(): pl.pallas_call(kernel, out_shape=[jax.ShapeDtypeStruct((8, 128), F32), ja...  56.1 us

profile of v5, /device:TPU:1, one launch (start us, length us, event | category | flops | bytes accessed | tf_op | source)
XLA Modules:
  0.0 58.5 jit_solution(284664296783536955)
XLA Ops:
  0.6 56.1 %score_and_update.1 = (f32[8,128]{1,0:T(8,128)S(1)}, f32[512,512]{1,0:T(8,128)S(1)}, f32[1,512]{1,0:T(1,128)S(1)}) custom-call(bf16[1024,128]{1,0:T(8,128)(2,1)} %emb.1, bf16[512,4096]{1,0:T(8,128)(2,1)} %cen.1, s32[8,128]{1,0:T(8,128)} %bitcast.6, s32[1,512]{1,0:T(1,128)} %bitcast.7), custom_call_target="tpu_custom_call" | custom-call | tf_op jit(solution)/shard_map/score_and_update/pallas_call | solution.py:469
  56.8 1.1 %broadcast_divide_fusion = f32[512,512]{1,0:T(8,128)} fusion(f32[512,512]{1,0:T(8,128)S(1)} %get-tuple-element.6, f32[512]{0:T(512)S(1)} %bitcast.5), kind=kLoop, calls=%fused_computation | loop fusion | flops 262144 | bytes 2099200 | tf_op jit(solution)/shard_map/div | solution.py:508
  57.9 0.6 %copy.7 = f32[1024]{0:T(1024)} copy(f32[1024]{0:T(1024)S(1)} %bitcast.4) | data formatting | bytes 8192

commit v6 on v5

--- a/solution.py
+++ b/solution.py
@@ -15,7 +15,7 @@
 HEAD = 480
 STAGES = 0, 384, 640, 1024
 QUART = CENT // NX
-PIECES = 8
+PIECES = 4
 PIECE = QUART // PIECES
 SLOT_Y = (0, 3, 1, 2)
 F32, BF16 = jnp.float32, jnp.bfloat16

time: 58.5 us -> 57.3 us (0.979)
  Pallas kernels: 56.1 us -> 54.7 us
    pallas_call x1, Pallas kernels: 56.1 us -> 54.7 us  [on_device(): pl.pallas_call(kernel, out_shape=[jax.ShapeDtypeStruct((8, 128), F32), ja...]
where the time goes in v6:
time: 57.3 us; the launch traced here: 57 us
  Pallas kernels  54.7 us (95%)
  other arithmetic  1.11 us (2%)
  between operations  0.64 us (1%)
  local copies, waits for them, and re-layouts  0.59 us (1%)
    pallas_call x1, Pallas kernels, on_device(): pl.pallas_call(kernel, out_shape=[jax.ShapeDtypeStruct((8, 128), F32), ja...  54.7 us

profile of v6, /device:TPU:1, one launch (start us, length us, event | category | flops | bytes accessed | tf_op | source)
XLA Modules:
  0.0 57.0 jit_solution(15583513952813363294)
XLA Ops:
  0.6 54.7 %score_and_update.1 = (f32[8,128]{1,0:T(8,128)S(1)}, f32[512,512]{1,0:T(8,128)S(1)}, f32[1,512]{1,0:T(1,128)S(1)}) custom-call(bf16[1024,128]{1,0:T(8,128)(2,1)} %emb.1, bf16[512,4096]{1,0:T(8,128)(2,1)} %cen.1, s32[8,128]{1,0:T(8,128)} %bitcast.6, s32[1,512]{1,0:T(1,128)} %bitcast.7), custom_call_target="tpu_custom_call" | custom-call | tf_op jit(solution)/shard_map/score_and_update/pallas_call | solution.py:469
  55.3 1.1 %broadcast_divide_fusion = f32[512,512]{1,0:T(8,128)} fusion(f32[512,512]{1,0:T(8,128)S(1)} %get-tuple-element.6, f32[512]{0:T(512)S(1)} %bitcast.5), kind=kLoop, calls=%fused_computation | loop fusion | flops 262144 | bytes 2099200 | tf_op jit(solution)/shard_map/div | solution.py:508
  56.5 0.6 %copy.7 = f32[1024]{0:T(1024)} copy(f32[1024]{0:T(1024)S(1)} %bitcast.4) | data formatting | bytes 8192
